TPU v7x, 256 devices: a whole 4x4x8 slice. The times are simulated.
256 devices in a mesh: dp: 16 (over z, core), head: 16 (over y, x).
Axes of the slice: x: 4, y: 4, z: 8, core: 2. Of those that a mesh axis runs over, the one named last changes fastest.
Arguments:
- states: bfloat16 [8192, 8192], P('dp', 'head'), may hold values from -1000 to 1000
- gain: float32 [8192], P('head'), may hold values from 0.25 to 1.75
- kv_weight: bfloat16 [8192, 2048], P('head'), may hold values from -0.0625 to 0.0625
- kv_bias: float32 [2048], P('head'), may hold values from -3 to 3
- sketch: int32 [2048, 512], P('head'), may hold values from -1 to 1
Outputs:
- basis: float32 [2048, 512], P('head')
- latent: float32 [8192, 512], P('dp', 'head')
All inputs are finite; a program needn't handle non-finite values.
Results may differ from a plain program's by a relative error of at most 0.0065.
Values may be sent and summed in bfloat16 or wider, within the bound.
A program may use at most 64 MiB of HBM per device.

v0:
```python
import jax
import jax.numpy as jnp
from jax import lax
from jax.sharding import PartitionSpec as P

D = 8192
ITERS = 3


def local(states, gain, kv_weight, kv_bias, sketch):
    values = states.astype(jnp.float32)
    local_squares = jnp.sum(values * values, axis=1)
    total_squares = lax.psum(local_squares, "head")
    scale = lax.rsqrt(total_squares / D + 1e-06)
    normed = (values * scale[:, None] * gain[None, :]).astype(jnp.bfloat16)
    own_columns = lax.all_to_all(kv_weight, "head", split_axis=1, concat_axis=0, tiled=True)
    summed = jnp.einsum(
        "dc,rd->cr",
        own_columns,
        lax.all_gather(normed, "head", axis=1, tiled=True),
        preferred_element_type=jnp.float32,
    )
    kv_local = (summed + kv_bias[:, None]).astype(jnp.bfloat16)
    kv_float = kv_local.astype(jnp.float32)
    basis = sketch.astype(jnp.float32)
    contract = (((0,), (0,)), ((), ()))
    for step in range(ITERS):
        partial_value = lax.dot_general(kv_float, basis, contract, precision=lax.Precision.HIGHEST)
        products = lax.psum(partial_value, "head")
        column_part = jnp.dot(kv_float, products, precision=lax.Precision.HIGHEST)
        columns = lax.psum(column_part, "dp")
        gram_part = lax.dot_general(columns, columns, contract, precision=lax.Precision.HIGHEST)
        gram = lax.psum(gram_part, "head")
        lower = jnp.linalg.cholesky(gram)
        basis = lax.linalg.triangular_solve(
            lower, columns, left_side=False, lower=True, transpose_a=True
        )
    final = lax.dot_general(kv_float, basis, contract, precision=lax.Precision.HIGHEST)
    latent = lax.psum_scatter(final, "head", scatter_dimension=1, tiled=True)
    return (basis, latent)


def solution(mesh):
    in_specs = (P("dp", "head"), P("head"), P("head", None), P("head"), P("head", None))
    out_specs = (P("head", None), P("dp", "head"))
    return jax.shard_map(local, mesh=mesh, in_specs=in_specs, out_specs=out_specs, check_vma=False)
```

profile of v0, /device:TPU:1, one launch (start us, length us, event | category | flops | bytes accessed | tf_op | source)
XLA Modules:
  0.0 1573.9 jit_solution(16369414879871344131)
XLA Ops:
  8.6 34.3 %psum.70 = f32[512]{0:T(512)S(1)} all-reduce(f32[512]{0:T(512)S(1)} %fusion.1), channel_id=1, replica_groups=mesh['dp'=16,'head'=16] {'head'}, use_global_device_ids=true, to_apply=%region_1.0 | all-reduce | flops 512 | bytes 4096 | tf_op jit(solution)/shard_map/psum | solution.py:13
  45.0 2.6 copy.21
  47.5 26.9 %all_to_all.19 = bf16[512,16,128]{0,2,1:T(8,128)(2,1)S(1)} all-to-all(bf16[512,16,128]{0,2,1:T(8,128)(2,1)} %bitcast.169), channel_id=1, replica_groups=mesh['dp'=16,'head'=16] {'head'}, dimensions={1} | all-to-all | bytes 4194304 | tf_op jit(solution)/shard_map/all_to_all | solution.py:16
  76.8 67.4 %all-gather.2.cloned.1.call-done = bf16[512,8192]{1,0:T(8,128)(2,1)} async-done(((bf16[512,512]{1,0:T(8,128)(2,1)}), bf16[512,8192]{1,0:T(8,128)(2,1)}) %all-gather.2.cloned.1.call-update) | async-done | bytes 8388624 | tf_op jit(solution)/shard_map/all_gather | solution.py:20
  144.2 6.4 fusion
  152.3 96.1 %all-reduce.11.cloned.1.call-done = f32[512,512]{1,0:T(8,128)} async-done(((f32[512,512]{1,0:T(8,128)}), f32[512,512]{1,0:T(8,128)}) %all-reduce.11.cloned.1.call-update) | async-done | bytes 1048592 | tf_op jit(solution)/shard_map/psum | solution.py:29
  248.5 2.4 fusion.134
  251.0 109.7 %all-reduce.13.cloned.1.call-done = f32[128,512]{1,0:T(8,128)} async-done(((f32[128,512]{1,0:T(8,128)}), f32[128,512]{1,0:T(8,128)}) %all-reduce.13.cloned.1.call-update) | async-done | bytes 262160 | tf_op jit(solution)/shard_map/psum | solution.py:31
  360.7 3.1 fusion.135
  364.1 96.1 %all-reduce.15.cloned.1.call-done = f32[512,512]{0,1:T(8,128)} async-done(((f32[512,512]{0,1:T(8,128)}), f32[512,512]{0,1:T(8,128)}) %all-reduce.15.cloned.1.call-update) | async-done | bytes 1048592 | tf_op jit(solution)/shard_map/psum | solution.py:33
  462.1 11.7 cholesky.374
  473.9 9.8 custom-call.31
  484.5 11.7 cholesky.393
  496.2 10.2 custom-call.32
  507.1 11.7 cholesky.414
  519.6 9.8 custom-call.33
  530.0 11.7 cholesky.431
  546.0 8.1 while.6
  554.1 39.3 %custom-call.34 = f32[4,128,128]{1,2,0:T(8,128)S(1)} custom-call(f32[4,128,128]{2,1,0:T(8,128)S(1)} %get-tuple-element.24), custom_call_target="InvertDiagBlocksLowerTriangular" | custom-call | tf_op jit(solution)/shard_map/triangular_solve/custom-call.3 | solution.py:35
  597.5 96.5 %all-reduce.17.cloned.1.call-done = f32[512,512]{1,0:T(8,128)} async-done(((f32[512,512]{1,0:T(8,128)}), f32[512,512]{1,0:T(8,128)}) %all-reduce.17.cloned.1.call-update) | async-done | bytes 1048592 | tf_op jit(solution)/shard_map/psum | solution.py:29
  694.0 2.4 fusion.136
  696.6 109.6 %all-reduce.19.cloned.1.call-done = f32[128,512]{1,0:T(8,128)} async-done(((f32[128,512]{1,0:T(8,128)}), f32[128,512]{1,0:T(8,128)}) %all-reduce.19.cloned.1.call-update) | async-done | bytes 262160 | tf_op jit(solution)/shard_map/psum | solution.py:31
  806.2 3.1 fusion.137
  809.4 96.2 %all-reduce.21.cloned.1.call-done = f32[512,512]{0,1:T(8,128)} async-done(((f32[512,512]{0,1:T(8,128)}), f32[512,512]{0,1:T(8,128)}) %all-reduce.21.cloned.1.call-update) | async-done | bytes 1048592 | tf_op jit(solution)/shard_map/psum | solution.py:33
  907.5 11.7 cholesky.446
  919.3 9.8 custom-call.35
  929.8 11.7 cholesky.465
  942.9 10.2 custom-call.36
  953.8 11.7 cholesky.486
  966.2 9.8 custom-call.37
  976.6 11.7 cholesky.503
  992.0 8.1 while.7
  1000.1 39.3 %custom-call.38 = f32[4,128,128]{1,2,0:T(8,128)S(1)} custom-call(f32[4,128,128]{2,1,0:T(8,128)S(1)} %get-tuple-element.25), custom_call_target="InvertDiagBlocksLowerTriangular" | custom-call | tf_op jit(solution)/shard_map/triangular_solve/custom-call.3 | solution.py:35
  1043.5 96.5 %all-reduce.23.cloned.1.call-done = f32[512,512]{1,0:T(8,128)} async-done(((f32[512,512]{1,0:T(8,128)}), f32[512,512]{1,0:T(8,128)}) %all-reduce.23.cloned.1.call-update) | async-done | bytes 1048592 | tf_op jit(solution)/shard_map/psum | solution.py:29
  1140.0 2.4 fusion.138
  1142.5 109.7 %all-reduce.25.cloned.1.call-done = f32[128,512]{1,0:T(8,128)} async-done(((f32[128,512]{1,0:T(8,128)}), f32[128,512]{1,0:T(8,128)}) %all-reduce.25.cloned.1.call-update) | async-done | bytes 262160 | tf_op jit(solution)/shard_map/psum | solution.py:31
  1252.2 3.1 fusion.139
  1255.4 96.3 %all-reduce.27.cloned.1.call-done = f32[512,512]{0,1:T(8,128)} async-done(((f32[512,512]{0,1:T(8,128)}), f32[512,512]{0,1:T(8,128)}) %all-reduce.27.cloned.1.call-update) | async-done | bytes 1048592 | tf_op jit(solution)/shard_map/psum | solution.py:33
  1353.6 11.7 cholesky.518
  1365.5 9.8 custom-call.39
  1376.0 11.7 cholesky.537
  1389.1 10.0 custom-call.40
  1399.8 11.7 cholesky.558
  1412.2 9.8 custom-call.41
  1422.6 11.7 cholesky.575
  1437.9 8.5 while.8
  1446.4 39.3 %custom-call.42 = f32[4,128,128]{1,2,0:T(8,128)S(1)} custom-call(f32[4,128,128]{2,1,0:T(8,128)S(1)} %get-tuple-element.26), custom_call_target="InvertDiagBlocksLowerTriangular" | custom-call | tf_op jit(solution)/shard_map/triangular_solve/custom-call.3 | solution.py:35
  1490.6 76.4 %reduce-scatter.2.cloned.1.call-done = f32[512,32]{0,1:T(8,128)} async-done(((f32[512,512]{0,1:T(8,128)}), f32[512,32]{0,1:T(8,128)}) %reduce-scatter.2.cloned.1.call-update) | async-done | bytes 65552 | tf_op jit(solution)/shard_map/reduce_scatter | solution.py:39
  (174 shorter events, 66.0 us)
Async XLA Ops:
  7.2 37.8 %copy-start.6 = (bf16[512,2048]{1,0:T(8,128)(2,1)S(1)}, bf16[512,2048]{1,0:T(8,128)(2,1)}, u32[]{:S(2)}) copy-start(bf16[512,2048]{1,0:T(8,128)(2,1)} %param.10) | copy-start | bytes 6291460
  7.2 137.1 %all-gather.2.cloned.1.call-start = ((), (), s32[]{:S(2)}) async-start(), calls=%async_computation.2 | async-start | bytes 8912896 | tf_op jit(solution)/shard_map/all_gather | solution.py:20
  44.9 203.6 %all-reduce.11.cloned.1.call-start = ((), (), s32[]{:S(2)}) async-start(), calls=%async_computation.3 | async-start | bytes 2097152 | tf_op jit(solution)/shard_map/psum | solution.py:29
  74.4 69.8 %copy-start.8 = (f32[128]{0:T(128)S(1)}, f32[128]{0:T(128)}, u32[]{:S(2)}) copy-start(f32[128]{0:T(128)} %param.11) | copy-start | bytes 1540
  144.2 6.4 copy-start.7
  152.3 208.4 %all-reduce.13.cloned.1.call-start = ((), (), s32[]{:S(2)}) async-start(), calls=%async_computation.4 | async-start | bytes 524288 | tf_op jit(solution)/shard_map/psum | solution.py:31
  250.9 209.2 %all-reduce.15.cloned.1.call-start = ((), (), s32[]{:S(2)}) async-start(), calls=%async_computation.5 | async-start | bytes 2097152 | tf_op jit(solution)/shard_map/psum | solution.py:33
  363.8 330.2 %all-reduce.17.cloned.1.call-start = ((), (), s32[]{:S(2)}) async-start(), calls=%async_computation.6 | async-start | bytes 2097152 | tf_op jit(solution)/shard_map/psum | solution.py:29
  460.2 1.7 copy-start
  507.1 86.3 %copy-start.3 = (f32[128,512]{1,0:T(8,128)S(1)}, f32[128,512]{1,0:T(8,128)}, u32[]{:S(2)}) copy-start(f32[128,512]{1,0:T(8,128)} %all-reduce.13.cloned.1.call-done) | copy-start | bytes 786436
  597.5 208.7 %all-reduce.19.cloned.1.call-start = ((), (), s32[]{:S(2)}) async-start(), calls=%async_computation.7 | async-start | bytes 524288 | tf_op jit(solution)/shard_map/psum | solution.py:31
  696.5 209.0 %all-reduce.21.cloned.1.call-start = ((), (), s32[]{:S(2)}) async-start(), calls=%async_computation.8 | async-start | bytes 2097152 | tf_op jit(solution)/shard_map/psum | solution.py:33
  809.3 330.7 %all-reduce.23.cloned.1.call-start = ((), (), s32[]{:S(2)}) async-start(), calls=%async_computation.9 | async-start | bytes 2097152 | tf_op jit(solution)/shard_map/psum | solution.py:29
  905.6 1.7 copy-start.1
  953.8 85.6 %copy-start.5 = (f32[128,512]{1,0:T(8,128)S(1)}, f32[128,512]{1,0:T(8,128)}, u32[]{:S(2)}) copy-start(f32[128,512]{1,0:T(8,128)} %all-reduce.19.cloned.1.call-done) | copy-start | bytes 786436
  1043.5 208.8 %all-reduce.25.cloned.1.call-start = ((), (), s32[]{:S(2)}) async-start(), calls=%async_computation.10 | async-start | bytes 524288 | tf_op jit(solution)/shard_map/psum | solution.py:31
  1142.5 209.2 %all-reduce.27.cloned.1.call-start = ((), (), s32[]{:S(2)}) async-start(), calls=%async_computation.11 | async-start | bytes 2097152 | tf_op jit(solution)/shard_map/psum | solution.py:33
  1255.3 311.6 %reduce-scatter.2.cloned.1.call-start = ((), (), s32[]{:S(2)}) async-start(), calls=%async_computation.12 | async-start | bytes 1114112 | tf_op jit(solution)/shard_map/reduce_scatter | solution.py:39
  1351.7 1.7 copy-start.2
  1399.8 86.0 %copy-start.4 = (f32[128,512]{1,0:T(8,128)S(1)}, f32[128,512]{1,0:T(8,128)}, u32[]{:S(2)}) copy-start(f32[128,512]{1,0:T(8,128)} %all-reduce.25.cloned.1.call-done) | copy-start | bytes 786436
Sparse Core Ops, SparseCore 0:
  45.0 99.1 all-gather.1
  152.4 96.0 all-reduce.10
  251.4 109.2 all-reduce.12
  364.1 96.0 all-reduce.14
  597.6 96.3 all-reduce.16
  696.9 109.2 all-reduce.18
  809.4 96.0 all-reduce.20
  1043.6 96.3 all-reduce.22
  1142.9 109.2 all-reduce.24
  1255.6 96.0 all-reduce.26
  1489.9 77.0 reduce-scatter.1
where the time goes:
time: 1580 us; the launch traced here: 1570 us
  waiting for transfers between devices  1050 us (66%)
  other arithmetic  361 us (23%)
  blocking collectives  61.1 us (4%)
  matrix products  42 us (3%)
  local copies, waits for them, and re-layouts  35.8 us (2%)
  between operations  22.6 us (1%)
    psum x3, waiting for transfers between devices, local(): columns = lax.psum(column_part, 'dp')  329 us
    psum x3, waiting for transfers between devices, local(): products = lax.psum(partial_value, 'head')  289 us
    psum x3, waiting for transfers between devices, local(): gram = lax.psum(gram_part, 'head')  289 us
    another operation x44, other arithmetic, local(): lower = jnp.linalg.cholesky(gram)  238 us
    another operation x8, other arithmetic, local(): lax.linalg.triangular_solve(lower, columns, left_side=False, lower=True,...  119 us
    reduce_scatter x1, waiting for transfers between devices, local(): latent = lax.psum_scatter(final, 'head', scatter_dimension=1, tiled=True)  76.4 us
    all_gather x1, waiting for transfers between devices, local(): lax.all_gather(normed, 'head', axis=1, tiled=True)  67.4 us
    psum x1, blocking collectives, local(): total_squares = lax.psum(local_squares, 'head')  34.3 us
  transfers between devices with their start and end apart: 11, of which 11 were waited for; matrix products, arithmetic and copies ran while one was open for 0% of the time, Pallas kernels for 0%

commit v1 on v0

v1 whole, which is shorter than its diff:
```python
import functools

import jax
import jax.numpy as jnp
from jax import lax
from jax.experimental import pallas as pl
from jax.experimental.pallas import tpu as pltpu
from jax.sharding import PartitionSpec as P

D = 8192
F32 = jnp.float32
BF16 = jnp.bfloat16
MESH = pl.DeviceIdType.MESH
VM = pl.BlockSpec(memory_space=pltpu.VMEM)
DMA = pltpu.SemaphoreType.DMA


def position():
    dp, head = lax.axis_index("dp"), lax.axis_index("head")
    return dp, head, dp // 2, dp % 2, head // 4, head % 4


def greet(devices):
    barrier = pltpu.get_barrier_semaphore()
    for device in devices:
        pl.semaphore_signal(barrier, inc=1, device_id=device, device_id_type=MESH)
    pl.semaphore_wait(barrier, len(devices))


class Copies:
    def __init__(self, send_sem, recv_sem):
        self.send_sem, self.recv_sem, self.started = send_sem, recv_sem, []

    def go(self, src, dst, device):
        n = len(self.started)
        copy = pltpu.make_async_remote_copy(
            src_ref=src, dst_ref=dst, send_sem=self.send_sem.at[n],
            recv_sem=self.recv_sem.at[n], device_id=device, device_id_type=MESH,
        )
        copy.start()
        self.started.append(copy)
        return copy

    def finish(self):
        for copy in self.started:
            copy.wait_send()


def params(collective_id=None, mib=48):
    if collective_id is None:
        return pltpu.CompilerParams(vmem_limit_bytes=mib << 20)
    return pltpu.CompilerParams(
        collective_id=collective_id, has_side_effects=True, vmem_limit_bytes=mib << 20
    )


def dot(a, b, dims, precision=None):
    return lax.dot_general(a, b, (dims, ((), ())), precision=precision, preferred_element_type=F32)


NN, NT, TN = ((1,), (0,)), ((1,), (1,)), ((0,), (0,))
HI = lax.Precision.HIGHEST


def split(v):
    high = v.astype(BF16)
    return high, (v - high.astype(F32)).astype(BF16)


def dot3(a, b, dims):
    return dot(a[0], b[0], dims) + (dot(a[0], b[1], dims) + dot(a[1], b[0], dims))


def kv_kernel(st_ref, gain_ref, w_ref, bias_ref, kv_ref, sq_ref, n_ref, own_a, own_b, send_a,
              recv_a, send_b, recv_b, recv2_a, recv2_b, send_sem, recv_sem):
    dp, head, _, _, y, x = position()
    others = [lax.rem(head + k, 16) for k in range(1, 16)]
    xs = [lax.rem(x + k, 4) for k in (1, 2, 3)]
    ys = [lax.rem(y + k, 4) for k in (1, 2, 3)]
    to_x = [(dp, y * 4 + v) for v in xs]
    to_y = [(dp, v * 4 + x) for v in ys]
    copies = Copies(send_sem, recv_sem)

    values = st_ref[...].astype(F32)
    squares = dot(jnp.ones((8, 512), F32), values * values, NT, HI)
    sq_ref[head] = squares
    greet([(dp, v) for v in others])
    arrivals = [copies.go(sq_ref.at[head], sq_ref.at[head], (dp, v)) for v in others]
    for copy in arrivals:
        copy.wait_recv()
    total = sq_ref[0]
    for k in range(1, 16):
        total = total + sq_ref[k]
    scale = lax.rsqrt(total / D + 1e-06)
    column = jnp.transpose(jnp.broadcast_to(scale[0:1], (128, 512)))
    for block in range(4):
        cols = pl.ds(128 * block, 128)
        part = st_ref[:, cols].astype(F32) * column * gain_ref[:, cols]
        n_ref[:, cols] = part.astype(BF16)

    def product(rows, owner):
        cols = pl.ds(pl.multiple_of(owner * 128, 128), 128)
        return dot(n_ref[rows], w_ref[:, cols], NN)

    low, high = pl.ds(0, 256), pl.ds(256, 256)
    first_a, first_b = [], []
    for k in range(3):
        for v in range(4):
            send_a[k, v] = product(low, v * 4 + xs[k]).astype(BF16)
        first_a.append(copies.go(send_a.at[k], recv_a.at[k], to_x[k]))
        for v in range(4):
            send_b[k, v] = product(high, ys[k] * 4 + v).astype(BF16)
        first_b.append(copies.go(send_b.at[k], recv_b.at[k], to_y[k]))
    for v in range(4):
        own_a[v] = product(low, v * 4 + x)
        own_b[v] = product(high, y * 4 + v)
    second_a, second_b = [], []
    for copy in first_a:
        copy.wait_recv()
    for v in range(4):
        own_a[v] += (recv_a[0, v].astype(F32) + recv_a[1, v].astype(F32)) + recv_a[2, v].astype(F32)
    for k in range(3):
        second_a.append(copies.go(own_a.at[ys[k]], recv2_a.at[k], to_y[k]))
    for copy in first_b:
        copy.wait_recv()
    for v in range(4):
        own_b[v] += (recv_b[0, v].astype(F32) + recv_b[1, v].astype(F32)) + recv_b[2, v].astype(F32)
    for k in range(3):
        second_b.append(copies.go(own_b.at[xs[k]], recv2_b.at[k], to_x[k]))
    for copy in second_a:
        copy.wait_recv()
    summed = own_a[y] + (recv2_a[0] + recv2_a[1]) + recv2_a[2]
    kv_ref[y, x, low] = (summed + bias_ref[...]).astype(BF16)
    third_a = [copies.go(kv_ref.at[y, x, low], kv_ref.at[y, x, low], d) for d in to_x]
    for copy in second_b:
        copy.wait_recv()
    summed = own_b[x] + (recv2_b[0] + recv2_b[1]) + recv2_b[2]
    kv_ref[y, x, high] = (summed + bias_ref[...]).astype(BF16)
    third_b = [copies.go(kv_ref.at[y, x, high], kv_ref.at[y, x, high], d) for d in to_y]
    for copy in third_a:
        copy.wait_recv()
    last = [copies.go(kv_ref.at[y, :, low], kv_ref.at[y, :, low], d) for d in to_y]
    for copy in third_b:
        copy.wait_recv()
    last += [copies.go(kv_ref.at[:, x, high], kv_ref.at[:, x, high], d) for d in to_x]
    for copy in last:
        copy.wait_recv()
    copies.finish()


def make_kv(states, gain, weight, bias):
    n = 15 + 6 + 6 + 6 + 6
    return pl.pallas_call(
        kv_kernel,
        out_shape=jax.ShapeDtypeStruct((4, 4, 512, 128), BF16),
        in_specs=[VM] * 4,
        out_specs=VM,
        scratch_shapes=[
            pltpu.VMEM((16, 8, 512), F32),
            pltpu.VMEM((512, 512), BF16),
            pltpu.VMEM((4, 256, 128), F32),
            pltpu.VMEM((4, 256, 128), F32),
            pltpu.VMEM((3, 4, 256, 128), BF16),
            pltpu.VMEM((3, 4, 256, 128), BF16),
            pltpu.VMEM((3, 4, 256, 128), BF16),
            pltpu.VMEM((3, 4, 256, 128), BF16),
            pltpu.VMEM((3, 256, 128), F32),
            pltpu.VMEM((3, 256, 128), F32),
            DMA((n,)),
            DMA((n,)),
        ],
        compiler_params=params(1),
        cost_estimate=pl.CostEstimate(flops=1 << 31, bytes_accessed=100 << 20, transcendentals=0),
    )(states, gain.reshape(1, 512), weight, bias.reshape(1, 128))


def corr_kernel(kv_ref, g_ref, part, recv_half, recv_z, send_sem, recv_sem):
    dp, head, z, c, y, x = position()
    sibling = (dp + 1 - 2 * c, head)
    zs = [lax.rem(z + k, 8) for k in range(1, 8)]
    to_z = [(v * 2 + c, head) for v in zs]
    copies = Copies(send_sem, recv_sem)
    greet([sibling] + to_z)
    for block in range(16):
        part[block // 8, block % 8] = dot(kv_ref[y, x], kv_ref[block // 4, block % 4], TN)
    to_sibling = copies.go(part.at[1 - c], recv_half, sibling)
    to_sibling.wait_recv()
    for block in range(8):
        part[c, block] += recv_half[block]
    first = [copies.go(part.at[c, zs[k]], recv_z.at[k], to_z[k]) for k in range(7)]
    total = part[c, z]
    for k in range(7):
        first[k].wait_recv()
        total = total + recv_z[k]

    def place(owner, half):
        return pl.ds(pl.multiple_of((half * 8 + owner) * 128, 128), 128)

    mine = place(z, c)
    g_ref[:, mine] = total
    second = [copies.go(g_ref.at[:, mine], g_ref.at[:, mine], d) for d in to_z]
    last = [copies.go(g_ref.at[:, mine], g_ref.at[:, mine], sibling)]
    for k in range(7):
        second[k].wait_recv()
        there = place(lax.rem(z + 7 - k, 8), c)
        last.append(copies.go(g_ref.at[:, there], g_ref.at[:, there], sibling))
    for copy in last:
        copy.wait_recv()
    copies.finish()


def make_corr(kv):
    n = 1 + 7 + 7 + 8
    return pl.pallas_call(
        corr_kernel,
        out_shape=jax.ShapeDtypeStruct((128, 2048), F32),
        in_specs=[VM],
        out_specs=VM,
        scratch_shapes=[
            pltpu.VMEM((2, 8, 128, 128), F32),
            pltpu.VMEM((8, 128, 128), F32),
            pltpu.VMEM((7, 128, 128), F32),
            DMA((n,)),
            DMA((n,)),
        ],
        compiler_params=params(2),
    )(kv)


def gather_kernel(x_ref, o_ref, send_sem, recv_sem, own_sem):
    dp, head, _, c, y, x = position()
    rows = x_ref.shape[0]
    quarter = rows // 4
    xs = [lax.rem(x + k, 4) for k in (1, 2, 3)]
    ys = [lax.rem(y + k, 4) for k in (1, 2, 3)]
    to_x = [(dp, y * 4 + v) for v in xs]
    to_y = [(dp, v * 4 + x) for v in ys]
    sibling = (dp + 1 - 2 * c, head)
    copies = Copies(send_sem, recv_sem)
    greet(to_x + to_y + [sibling])
    own = pltpu.make_async_copy(x_ref, o_ref.at[y, x], own_sem)
    own.start()
    a = pl.ds(pl.multiple_of(c * 2 * quarter, quarter), quarter)
    b = pl.ds(pl.multiple_of((c * 2 + 1) * quarter, quarter), quarter)
    first_a = [copies.go(x_ref.at[a], o_ref.at[y, x, a], d) for d in to_x]
    first_b = [copies.go(x_ref.at[b], o_ref.at[y, x, b], d) for d in to_y]
    own.wait()
    for copy in first_a:
        copy.wait_recv()
    second_a = [copies.go(o_ref.at[y, :, a], o_ref.at[y, :, a], d) for d in to_y]
    for copy in first_b:
        copy.wait_recv()
    second_b = [copies.go(o_ref.at[:, x, b], o_ref.at[:, x, b], d) for d in to_x]
    last = []
    for k in range(3):
        vx, vy = lax.rem(x + 3 - k, 4), lax.rem(y + 3 - k, 4)
        last.append(copies.go(o_ref.at[y, vx, a], o_ref.at[y, vx, a], sibling))
        last.append(copies.go(o_ref.at[vy, x, b], o_ref.at[vy, x, b], sibling))
    for k in range(3):
        vx, vy = lax.rem(x + 3 - k, 4), lax.rem(y + 3 - k, 4)
        second_a[k].wait_recv()
        last.append(copies.go(o_ref.at[vy, :, a], o_ref.at[vy, :, a], sibling))
        second_b[k].wait_recv()
        last.append(copies.go(o_ref.at[:, vx, b], o_ref.at[:, vx, b], sibling))
    for copy in last:
        copy.wait_recv()
    copies.finish()


def gather(block, collective_id):
    rows, width = block.shape
    out = pl.pallas_call(
        gather_kernel,
        out_shape=jax.ShapeDtypeStruct((4, 4, rows, width), block.dtype),
        in_specs=[VM],
        out_specs=VM,
        scratch_shapes=[DMA((24,)), DMA((24,)), DMA],
        compiler_params=params(collective_id),
    )(block)
    return out.reshape(16 * rows, width)


def invert_block(a):
    shape = (8, 128)
    rows = [a[8 * g:8 * g + 8] for g in range(16)]
    lane = lax.broadcasted_iota(jnp.int32, shape, 1)
    sub = lax.broadcasted_iota(jnp.int32, shape, 0)
    inverse = [(lane == sub + 8 * g).astype(F32) for g in range(16)]
    for p in range(16):
        spread = [[jnp.broadcast_to(rows[g][:, 8 * p + c:8 * p + c + 1], shape) for g in range(p, 16)]
                  for c in range(8)]
        pivots = None
        for r in range(8):
            pivot = jnp.broadcast_to(spread[r][0][r:r + 1], shape)
            pivots = pivot if pivots is None else jnp.where(sub == r, pivot, pivots)
            recip = 1.0 / pivot
            row = jnp.broadcast_to(rows[p][r:r + 1], shape) * recip
            inverse_row = jnp.broadcast_to(inverse[p][r:r + 1], shape) * recip
            heads = {c: jnp.broadcast_to(spread[c][0][r:r + 1], shape) * recip for c in range(r + 1, 8)}
            for i in range(16 - p):
                if i == 0 and r == 7:
                    continue
                factor = spread[r][i]
                if i == 0:
                    factor = jnp.where(sub > r, factor, 0.0)
                for c in range(r + 1, 8):
                    spread[c][i] = spread[c][i] - factor * heads[c]
                rows[p + i] = rows[p + i] - factor * row
                inverse[p + i] = inverse[p + i] - factor * inverse_row
        inverse[p] = inverse[p] * lax.rsqrt(pivots)
    return jnp.concatenate(inverse, axis=0)


def gram_into(c_ref, a_ref):
    for p in range(4):
        rows = slice(128 * p, 128 * p + 128)
        a_ref[rows, :128 * p + 128] = dot(c_ref[:, rows], c_ref[:, :128 * p + 128], TN, HI)


def invert_factor(a_ref, l_ref, inv_ref):
    inv_ref[...] = jnp.zeros_like(inv_ref)
    for p in range(4):
        here = slice(128 * p, 128 * p + 128)
        block = invert_block(a_ref[here, here])
        if p > 0:
            before = slice(0, 128 * p)
            inv_ref[here, before] = -dot(block, dot(l_ref[here, before], inv_ref[before, before], NN, HI), NN, HI)
        inv_ref[here, here] = block
        if p < 3:
            rest = slice(128 * p + 128, 512)
            panel = dot(a_ref[rest, here], block, NT, HI)
            l_ref[rest, here] = panel
            a_ref[rest, rest] -= dot(panel, panel, NT, HI)


def first_kernel(g_ref, s_ref, o_ref):
    g = split(g_ref[...])
    s = s_ref[...]
    o_ref[...] = dot(g[0], s, NN) + dot(g[1], s, NN)


def first_columns(corr, sketch):
    return pl.pallas_call(
        first_kernel, out_shape=jax.ShapeDtypeStruct((128, 512), F32),
        in_specs=[VM] * 2, out_specs=VM, compiler_params=params(),
    )(corr, sketch)


def step_kernel(c_ref, g_ref, o_ref, a_ref, l_ref, inv_ref, qh_ref, ql_ref):
    gram_into(c_ref, a_ref)
    invert_factor(a_ref, l_ref, inv_ref)
    for p in range(4):
        rows = slice(128 * p, 128 * p + 128)
        upto = slice(0, 128 * p + 128)
        high, low = split(dot3(split(c_ref[:, upto]), split(inv_ref[rows, upto]), NT))
        qh_ref[:, rows] = high
        ql_ref[:, rows] = low
    o_ref[...] = dot3(split(g_ref[...]), (qh_ref[...], ql_ref[...]), NN)


SQUARE = pltpu.VMEM((512, 512), F32)


def step(columns, corr):
    return pl.pallas_call(
        step_kernel, out_shape=jax.ShapeDtypeStruct((128, 512), F32),
        in_specs=[VM] * 2, out_specs=VM,
        scratch_shapes=[SQUARE] * 3 + [pltpu.VMEM((2048, 512), BF16)] * 2,
        compiler_params=params(),
    )(columns, corr)


def last_kernel(c_ref, own_ref, kv_ref, basis_ref, latent_ref, a_ref, l_ref, inv_ref):
    head = lax.axis_index("head")
    gram_into(c_ref, a_ref)
    invert_factor(a_ref, l_ref, inv_ref)
    basis_ref[...] = dot(own_ref[...], inv_ref[...], NT, HI)
    mine = inv_ref[pl.ds(pl.multiple_of(head * 32, 32), 32), :]
    high, low = split(dot(c_ref[...], mine, NT, HI))
    total = jnp.zeros((512, 32), F32)
    for block in range(16):
        rows = slice(128 * block, 128 * block + 128)
        kv = kv_ref[block // 4, block % 4]
        total = total + (dot(kv, high[rows], NN) + dot(kv, low[rows], NN))
    latent_ref[...] = total


def last(columns, own, kv):
    return pl.pallas_call(
        last_kernel,
        out_shape=(jax.ShapeDtypeStruct((128, 512), F32), jax.ShapeDtypeStruct((512, 32), F32)),
        in_specs=[VM] * 3, out_specs=(VM, VM),
        scratch_shapes=[SQUARE] * 3,
        compiler_params=params(),
    )(columns, own, kv)


def local(states, gain, kv_weight, kv_bias, sketch):
    whole_sketch = lax.all_gather(sketch.astype(BF16), "head", axis=0, tiled=True)
    kv = make_kv(states, gain, kv_weight, kv_bias)
    corr = make_corr(kv)
    own = first_columns(corr, whole_sketch)
    columns = gather(own, 3)
    own = step(columns, corr)
    columns = gather(own, 3)
    own = step(columns, corr)
    columns = gather(own, 3)
    return last(columns, own, kv)


def solution(mesh):
    in_specs = (P("dp", "head"), P("head"), P("head", None), P("head"), P("head", None))
    out_specs = (P("head", None), P("dp", "head"))
    return jax.shard_map(local, mesh=mesh, in_specs=in_specs, out_specs=out_specs, check_vma=False)
```

time: 1580 us -> 300 us (0.19)
  waiting for transfers between devices: 1050 us -> 0.04 us
  other arithmetic: 361 us -> 1.62 us
  Pallas kernels: 0 us -> 270 us
  blocking collectives: 61.1 us -> 0 us
  matrix products: 42 us -> 0 us
  local copies, waits for them, and re-layouts: 35.8 us -> 8.22 us
    psum x9 -> x0, waiting for transfers between devices: 907 us -> none  [the longest x3 329 us: local(): columns = lax.psum(column_part, 'dp')]
    another operation x52 -> x0, other arithmetic: 357 us -> none  [the longest x44 238 us: local(): lower = jnp.linalg.cholesky(gram)]
    pallas_call x0 -> x9, Pallas kernels: none -> 270 us  [the longest x3 74.9 us: gather(): pl.pallas_call(gather_kernel, out_shape=jax.ShapeDtypeStruct((4, 4, rows,...]
    reduce_scatter x1 -> x0, waiting for transfers between devices: 76.4 us -> none  [local(): latent = lax.psum_scatter(final, 'head', scatter_dimension=1, tiled=True)]
    all_gather x1, waiting for transfers between devices: 67.4 us -> 0.02 us  [local(): lax.all_gather(sketch.astype(BF16), 'head', axis=0, tiled=True)]
    psum x1 -> x0, blocking collectives: 34.3 us -> none  [local(): total_squares = lax.psum(local_squares, 'head')]
    dot_general x11 -> x0, matrix products: 29.4 us -> none  [the longest x3 9.26 us: local(): lax.dot_general(columns, columns, contract, precision=lax.Precision.HIGHEST)]
    all_to_all x1 -> x0, blocking collectives: 26.9 us -> none  [local(): lax.all_to_all(kv_weight, 'head', split_axis=1, concat_axis=0, tiled=True)]
  transfers between devices with their start and end apart: 11 -> 1, of which waited for: 11 -> 0; matrix products, arithmetic and copies ran while one was open for 0% -> 0% of each run, Pallas kernels for 0% -> 34%
where the time goes in v1:
time: 300 us; the launch traced here: 294 us
  Pallas kernels  270 us (90%)
  between operations  14.4 us (5%)
  local copies, waits for them, and re-layouts  8.22 us (3%)
    pallas_call x3, Pallas kernels, gather(): pl.pallas_call(gather_kernel, out_shape=jax.ShapeDtypeStruct((4, 4, rows,...  74.9 us
    pallas_call x1, Pallas kernels, make_kv(): pl.pallas_call(kv_kernel, out_shape=jax.ShapeDtypeStruct((4, 4, 512, 128)...  61.5 us
    pallas_call x2, Pallas kernels, step(): pl.pallas_call(step_kernel, out_shape=jax.ShapeDtypeStruct((128, 512), F3...  59.9 us
    pallas_call x1, Pallas kernels, make_corr(): pl.pallas_call(corr_kernel, out_shape=jax.ShapeDtypeStruct((128, 2048), F...  39.8 us
    pallas_call x1, Pallas kernels, last(): pl.pallas_call(last_kernel, out_shape=(jax.ShapeDtypeStruct((128, 512), F...  32.8 us
    unnamed x12, local copies, waits for them, and re-layouts  7.49 us
  transfers between devices with their start and end apart: 1, of which 0 were waited for; matrix products, arithmetic and copies ran while one was open for 0% of the time, Pallas kernels for 34%

profile of v1, /device:TPU:1, one launch (start us, length us, event | category | flops | bytes accessed | tf_op | source)
XLA Modules:
  0.0 293.9 jit_solution(382897728693278778)
XLA Ops:
  7.2 0.0 all-gather.2.cloned.1.call-start
  7.2 1.6 convert_element_type.3
  8.8 0.0 all-gather.2.cloned.1.call-update
  8.9 0.0 copy-start.2
  8.9 1.6 copy-done.2
  10.5 0.0 copy-start.3
  10.5 1.0 copy-done.3
  11.5 0.0 copy-start.4
  11.5 0.7 copy-done.4
  12.2 0.0 copy-start.5
  12.2 0.7 copy-done.5
  12.8 61.5 %shard_map.68.kv_ref = bf16[4,4,512,128]{3,2,1,0:T(8,128)(2,1)S(1)} custom-call(bf16[512,512]{1,0:T(8,128)(2,1)S(1)} %copy-done.3, f32[1,512]{1,0:T(1,128)S(1)} %bitcast.8, bf16[512,2048]{1,0:T(8,128)(2,1)S(1)} %copy-done.2, f32[1,128]{1,0:T(1,128)S(1)} %bitcast.9), custom_call_target="tpu_custom_call" | custom-call | flops 2147483648 | bytes 104857600 | tf_op jit(solution)/shard_map/pallas_call | solution.py:153
  74.4 39.8 %shard_map.69.g_ref = f32[128,2048]{1,0:T(8,128)S(1)} custom-call(bf16[4,4,512,128]{3,2,1,0:T(8,128)(2,1)S(1)} %shard_map.68.kv_ref), custom_call_target="tpu_custom_call" | custom-call | tf_op jit(solution)/shard_map/pallas_call | solution.py:214
  114.2 0.0 all-gather.2.cloned.1.call-done.s_ref
  114.2 0.0 copy-start.1
  114.3 1.6 copy-done.1
  115.8 0.7 shard_map.70.x_ref
  116.6 26.7 %shard_map.71 = f32[4,4,128,512]{3,2,1,0:T(8,128)S(1)} custom-call(f32[128,512]{1,0:T(8,128)S(1)} %shard_map.70.x_ref), custom_call_target="tpu_custom_call" | custom-call | tf_op jit(solution)/shard_map/pallas_call | solution.py:272
  143.3 29.9 %shard_map.72.x_ref = f32[128,512]{1,0:T(8,128)S(1)} custom-call(f32[2048,512]{1,0:T(8,128)S(1)} %bitcast.7, f32[128,2048]{1,0:T(8,128)S(1)} %shard_map.69.g_ref), custom_call_target="tpu_custom_call" | custom-call | tf_op jit(solution)/shard_map/pallas_call | solution.py:365
  173.2 24.8 %shard_map.73 = f32[4,4,128,512]{3,2,1,0:T(8,128)S(1)} custom-call(f32[128,512]{1,0:T(8,128)S(1)} %shard_map.72.x_ref), custom_call_target="tpu_custom_call" | custom-call | tf_op jit(solution)/shard_map/pallas_call | solution.py:272
  198.0 29.9 %shard_map.74.x_ref.own_ref = f32[128,512]{1,0:T(8,128)S(1)} custom-call(f32[2048,512]{1,0:T(8,128)S(1)} %bitcast.6, f32[128,2048]{1,0:T(8,128)S(1)} %shard_map.69.g_ref), custom_call_target="tpu_custom_call" | custom-call | tf_op jit(solution)/shard_map/pallas_call | solution.py:365
  228.0 23.3 %shard_map.75 = f32[4,4,128,512]{3,2,1,0:T(8,128)S(1)} custom-call(f32[128,512]{1,0:T(8,128)S(1)} %shard_map.74.x_ref.own_ref), custom_call_target="tpu_custom_call" | custom-call | tf_op jit(solution)/shard_map/pallas_call | solution.py:272
  251.4 0.0 copy-start
  251.4 1.9 copy-done
  253.3 32.8 %shard_map.76 = (f32[128,512]{1,0:T(8,128)}, f32[512,32]{1,0:T(8,128)S(1)}) custom-call(f32[2048,512]{1,0:T(8,128)} %bitcast.5, f32[128,512]{1,0:T(8,128)S(1)} %shard_map.74.x_ref.own_ref, bf16[4,4,512,128]{3,2,1,0:T(8,128)(2,1)S(1)} %shard_map.68.kv_ref), custom_call_target="tpu_custom_call" | custom-call | tf_op jit(solution)/shard_map/pallas_call | solution.py:389
  286.1 0.7 copy.7
Async XLA Ops:
  7.2 107.1 %all-gather.2.cloned.1.call-start = ((), (), s32[]{:S(2)}) async-start(), calls=%async_computation | async-start | bytes 2228224 | tf_op jit(solution)/shard_map/all_gather | solution.py:399
  8.9 1.6 copy-start.2
  10.5 1.0 copy-start.3
  11.5 0.7 copy-start.4
  12.2 0.7 copy-start.5
  114.2 1.6 copy-start.1
  251.4 1.9 copy-start
Sparse Core Ops, SparseCore 0:
  11.0 65.9 all-gather.1

commit v2 on v1

v2 whole, which is shorter than its diff:
```python
import jax
import jax.numpy as jnp
from jax import lax
from jax.experimental import pallas as pl
from jax.experimental.pallas import tpu as pltpu
from jax.sharding import PartitionSpec as P

D = 8192
F32 = jnp.float32
BF16 = jnp.bfloat16
MESH = pl.DeviceIdType.MESH
VM = pl.BlockSpec(memory_space=pltpu.VMEM)
DMA = pltpu.SemaphoreType.DMA


def position():
    dp, head = lax.axis_index("dp"), lax.axis_index("head")
    return dp, head, dp // 2, dp % 2, head // 4, head % 4


def greet(devices):
    barrier = pltpu.get_barrier_semaphore()
    for device in devices:
        pl.semaphore_signal(barrier, inc=1, device_id=device, device_id_type=MESH)
    pl.semaphore_wait(barrier, len(devices))


class Copies:
    def __init__(self, send_sem, recv_sem):
        self.send_sem, self.recv_sem, self.started = send_sem, recv_sem, []

    def go(self, src, dst, device):
        n = len(self.started)
        copy = pltpu.make_async_remote_copy(
            src_ref=src, dst_ref=dst, send_sem=self.send_sem.at[n],
            recv_sem=self.recv_sem.at[n], device_id=device, device_id_type=MESH,
        )
        copy.start()
        self.started.append(copy)
        return copy

    def finish(self):
        for copy in self.started:
            copy.wait_send()


def params(collective_id=None, mib=48):
    if collective_id is None:
        return pltpu.CompilerParams(vmem_limit_bytes=mib << 20)
    return pltpu.CompilerParams(
        collective_id=collective_id, has_side_effects=True, vmem_limit_bytes=mib << 20
    )


def dot(a, b, dims, precision=None):
    return lax.dot_general(a, b, (dims, ((), ())), precision=precision, preferred_element_type=F32)


NN, NT, TN = ((1,), (0,)), ((1,), (1,)), ((0,), (0,))
HI = lax.Precision.HIGHEST


def split(v):
    high = v.astype(BF16)
    return high, (v - high.astype(F32)).astype(BF16)


def kv_kernel(st_ref, gain_ref, w_ref, bias_ref, sketch_ref, kv_ref, whole_ref, sq_ref, n_ref, own_a, own_b,
              send_a, recv_a, send_b, recv_b, recv2_a, recv2_b, send_sem, recv_sem):
    dp, head, _, c, y, x = position()
    sibling = (dp + 1 - 2 * c, head)
    half = pl.ds(pl.multiple_of(c * 64, 64), 64)
    part_a = pl.ds(pl.multiple_of(c * 64, 32), 32)
    part_b = pl.ds(pl.multiple_of(c * 64 + 32, 32), 32)
    others = [lax.rem(head + k, 16) for k in range(1, 16)]
    xs = [lax.rem(x + k, 4) for k in (1, 2, 3)]
    ys = [lax.rem(y + k, 4) for k in (1, 2, 3)]
    to_x = [(dp, y * 4 + v) for v in xs]
    to_y = [(dp, v * 4 + x) for v in ys]
    copies = Copies(send_sem, recv_sem)

    values = st_ref[...].astype(F32)
    squares = dot(jnp.ones((8, 512), F32), values * values, NT, HI)
    sq_ref[head] = squares
    whole_ref[y, x, half] = sketch_ref[half].astype(BF16)
    greet([(dp, v) for v in others] + [sibling])
    arrivals = [copies.go(sq_ref.at[head], sq_ref.at[head], (dp, v)) for v in others]
    spread_a = [copies.go(whole_ref.at[y, x, part_a], whole_ref.at[y, x, part_a], d) for d in to_x]
    spread_b = [copies.go(whole_ref.at[y, x, part_b], whole_ref.at[y, x, part_b], d) for d in to_y]
    for copy in arrivals:
        copy.wait_recv()
    total = sq_ref[0]
    for k in range(1, 16):
        total = total + sq_ref[k]
    scale = lax.rsqrt(total / D + 1e-06)
    column = jnp.transpose(jnp.broadcast_to(scale[0:1], (128, 512)))
    for block in range(4):
        cols = pl.ds(128 * block, 128)
        part = st_ref[:, cols].astype(F32) * column * gain_ref[:, cols]
        n_ref[:, cols] = part.astype(BF16)

    def product(rows, owner):
        cols = pl.ds(pl.multiple_of(owner * 128, 128), 128)
        return dot(n_ref[rows], w_ref[:, cols], NN)

    for copy in spread_a + spread_b:
        copy.wait_recv()
    spread = [copies.go(whole_ref.at[y, :, part_a], whole_ref.at[y, :, part_a], d) for d in to_y]
    spread += [copies.go(whole_ref.at[:, x, part_b], whole_ref.at[:, x, part_b], d) for d in to_x]
    low, high = pl.ds(0, 256), pl.ds(256, 256)
    first_a, first_b = [], []
    for k in range(3):
        for v in range(4):
            send_a[k, v] = product(low, v * 4 + xs[k]).astype(BF16)
        first_a.append(copies.go(send_a.at[k], recv_a.at[k], to_x[k]))
        for v in range(4):
            send_b[k, v] = product(high, ys[k] * 4 + v).astype(BF16)
        first_b.append(copies.go(send_b.at[k], recv_b.at[k], to_y[k]))
    for v in range(4):
        own_a[v] = product(low, v * 4 + x)
        own_b[v] = product(high, y * 4 + v)
    second_a, second_b = [], []
    for copy in first_a:
        copy.wait_recv()
    for v in range(4):
        own_a[v] += (recv_a[0, v].astype(F32) + recv_a[1, v].astype(F32)) + recv_a[2, v].astype(F32)
    for k in range(3):
        second_a.append(copies.go(own_a.at[ys[k]], recv2_a.at[k], to_y[k]))
    for copy in first_b:
        copy.wait_recv()
    for v in range(4):
        own_b[v] += (recv_b[0, v].astype(F32) + recv_b[1, v].astype(F32)) + recv_b[2, v].astype(F32)
    for k in range(3):
        second_b.append(copies.go(own_b.at[xs[k]], recv2_b.at[k], to_x[k]))
    for copy in spread:
        copy.wait_recv()
    spread = [copies.go(whole_ref.at[:, :, half], whole_ref.at[:, :, half], sibling)]
    for copy in second_a:
        copy.wait_recv()
    summed = own_a[y] + (recv2_a[0] + recv2_a[1]) + recv2_a[2]
    kv_ref[y, x, low] = (summed + bias_ref[...]).astype(BF16)
    third_a = [copies.go(kv_ref.at[y, x, low], kv_ref.at[y, x, low], d) for d in to_x]
    for copy in second_b:
        copy.wait_recv()
    summed = own_b[x] + (recv2_b[0] + recv2_b[1]) + recv2_b[2]
    kv_ref[y, x, high] = (summed + bias_ref[...]).astype(BF16)
    third_b = [copies.go(kv_ref.at[y, x, high], kv_ref.at[y, x, high], d) for d in to_y]
    for copy in third_a:
        copy.wait_recv()
    last = [copies.go(kv_ref.at[y, :, low], kv_ref.at[y, :, low], d) for d in to_y]
    for copy in third_b:
        copy.wait_recv()
    last += [copies.go(kv_ref.at[:, x, high], kv_ref.at[:, x, high], d) for d in to_x]
    for copy in last + spread:
        copy.wait_recv()
    copies.finish()


def make_kv(states, gain, weight, bias, sketch):
    n = 15 + 6 + 6 + 6 + 6 + 13
    return pl.pallas_call(
        kv_kernel,
        out_shape=(
            jax.ShapeDtypeStruct((4, 4, 512, 128), BF16),
            jax.ShapeDtypeStruct((4, 4, 128, 512), BF16),
        ),
        in_specs=[VM] * 5,
        out_specs=(VM, VM),
        scratch_shapes=[
            pltpu.VMEM((16, 8, 512), F32),
            pltpu.VMEM((512, 512), BF16),
            pltpu.VMEM((4, 256, 128), F32),
            pltpu.VMEM((4, 256, 128), F32),
            pltpu.VMEM((3, 4, 256, 128), BF16),
            pltpu.VMEM((3, 4, 256, 128), BF16),
            pltpu.VMEM((3, 4, 256, 128), BF16),
            pltpu.VMEM((3, 4, 256, 128), BF16),
            pltpu.VMEM((3, 256, 128), F32),
            pltpu.VMEM((3, 256, 128), F32),
            DMA((n,)),
            DMA((n,)),
        ],
        compiler_params=params(1),
    )(states, gain.reshape(1, 512), weight, bias.reshape(1, 128), sketch)


def corr_kernel(kv_ref, g_ref, part, recv_half, recv_z, send_sem, recv_sem):
    dp, head, z, c, y, x = position()
    sibling = (dp + 1 - 2 * c, head)
    zs = [lax.rem(z + k, 8) for k in range(1, 8)]
    to_z = [(v * 2 + c, head) for v in zs]
    copies = Copies(send_sem, recv_sem)
    greet([sibling] + to_z)
    for block in range(16):
        cols = pl.ds(block % 2 * 128, 128)
        value = dot(kv_ref[y, x], kv_ref[block // 4, block % 4], TN)
        part[0, block // 2, :, cols] = value[:64]
        part[1, block // 2, :, cols] = value[64:]
    to_sibling = copies.go(part.at[1 - c], recv_half, sibling)
    to_sibling.wait_recv()
    for block in range(8):
        part[c, block] += recv_half[block]
    first = [copies.go(part.at[c, zs[k]], recv_z.at[k], to_z[k]) for k in range(7)]
    total = part[c, z]
    for k in range(7):
        first[k].wait_recv()
        total = total + recv_z[k]
    mine = pl.ds(pl.multiple_of(z * 256, 256), 256)
    g_ref[:, mine] = total
    second = [copies.go(g_ref.at[:, mine], g_ref.at[:, mine], d) for d in to_z]
    for copy in second:
        copy.wait_recv()
    copies.finish()


def make_corr(kv):
    n = 1 + 7 + 7
    return pl.pallas_call(
        corr_kernel,
        out_shape=jax.ShapeDtypeStruct((64, 2048), F32),
        in_specs=[VM],
        out_specs=VM,
        scratch_shapes=[
            pltpu.VMEM((2, 8, 64, 256), F32),
            pltpu.VMEM((8, 64, 256), F32),
            pltpu.VMEM((7, 64, 256), F32),
            DMA((n,)),
            DMA((n,)),
        ],
        compiler_params=params(2),
    )(kv)


def invert_block(a):
    shape = (8, 128)
    rows = [a[8 * g:8 * g + 8] for g in range(16)]
    lane = lax.broadcasted_iota(jnp.int32, shape, 1)
    sub = lax.broadcasted_iota(jnp.int32, shape, 0)
    inverse = [(lane == sub + 8 * g).astype(F32) for g in range(16)]
    for p in range(16):
        spread = [[jnp.broadcast_to(rows[g][:, 8 * p + c:8 * p + c + 1], shape) for g in range(p, 16)]
                  for c in range(8)]
        pivots = None
        for r in range(8):
            pivot = jnp.broadcast_to(spread[r][0][r:r + 1], shape)
            pivots = pivot if pivots is None else jnp.where(sub == r, pivot, pivots)
            recip = 1.0 / pivot
            row = jnp.broadcast_to(rows[p][r:r + 1], shape) * recip
            inverse_row = jnp.broadcast_to(inverse[p][r:r + 1], shape) * recip
            heads = {c: jnp.broadcast_to(spread[c][0][r:r + 1], shape) * recip for c in range(r + 1, 8)}
            for i in range(16 - p):
                if i == 0 and r == 7:
                    continue
                factor = spread[r][i]
                if i == 0:
                    factor = jnp.where(sub > r, factor, 0.0)
                for c in range(r + 1, 8):
                    spread[c][i] = spread[c][i] - factor * heads[c]
                rows[p + i] = rows[p + i] - factor * row
                inverse[p + i] = inverse[p + i] - factor * inverse_row
        inverse[p] = inverse[p] * lax.rsqrt(pivots)
    return jnp.concatenate(inverse, axis=0)


def order(t):
    r = t % 4
    return t + (r // 3) * (1 - t // 11) - (1 - (r + 3) // 4) * ((t + 11) // 12)


def beside(v):
    return jnp.concatenate(split(v), axis=1)


def halves(v):
    return v[:, :128] + v[:, 128:]


def quarters(v):
    rows = v.shape[0] // 2
    return halves(v[:rows]) + halves(v[rows:])


def iterate_kernel(g_ref, s_ref, kv_ref, basis_ref, latent_ref, cols_ref, q_ref, pair_ref, send_sem, recv_sem):
    dp, head, _, c, y, x = position()
    xs = [lax.rem(x + k, 4) for k in (1, 2, 3)]
    ys = [lax.rem(y + k, 4) for k in (1, 2, 3)]
    to_x = [(dp, y * 4 + v) for v in xs]
    to_y = [(dp, v * 4 + x) for v in ys]
    sibling = (dp + 1 - 2 * c, head)
    half = pl.ds(pl.multiple_of(c * 64, 64), 64)
    part_a = pl.ds(pl.multiple_of(c * 64, 32), 32)
    part_b = pl.ds(pl.multiple_of(c * 64 + 32, 32), 32)
    greet(to_x + to_y + [sibling])

    def copy(kp, n, where, device):
        here = cols_ref.at[(kp,) + where]
        return pltpu.make_async_remote_copy(
            src_ref=here, dst_ref=here, send_sem=send_sem.at[kp, n], recv_sem=recv_sem.at[kp, n],
            device_id=device, device_id_type=MESH,
        )

    every = slice(None)

    def first(kp):
        return [copy(kp, n, (y, x, part_a), to_x[n]) for n in range(3)] + [
            copy(kp, 3 + n, (y, x, part_b), to_y[n]) for n in range(3)]

    def second(kp):
        return [copy(kp, 6 + n, (y, every, part_a), to_y[n]) for n in range(3)] + [
            copy(kp, 9 + n, (every, x, part_b), to_x[n]) for n in range(3)]

    def third(kp):
        return [copy(kp, 12, (every, every, half), sibling)]

    def go(some):
        for one in some:
            one.start()

    def arrive(some):
        for one in some:
            one.wait_recv()

    def leave(some):
        for one in some:
            one.wait_send()

    pair_ref[:64], pair_ref[64:] = split(g_ref[...])
    for p in range(4):
        s = s_ref[:, :, :, 128 * p:128 * p + 128].reshape(2048, 128)
        new = dot(pair_ref[...], s, NN)
        cols_ref[p, y, x, half] = beside(new[:64] + new[64:])
        go(first(p))
    for p in range(4):
        arrive(first(p))
        go(second(p))
    arrive(second(0))
    go(third(0))

    def task(t, carry):
        kp = order(t)
        k, p = kp // 4, kp % 4
        arrive(third(kp))
        leave(first(kp) + second(kp) + third(kp))

        def subtract(q, carry):
            other = q_ref[k * 4 + q]
            now = cols_ref[kp].reshape(2048, 256)
            factor = beside(quarters(dot(other, now, TN)))
            weights = jnp.concatenate([factor, factor], axis=0)
            for r in range(4):
                rows = pl.ds(512 * r, 512)
                taken = halves(dot(q_ref[k * 4 + q, rows], weights, NN))
                old = cols_ref[kp, r].reshape(512, 256).astype(F32)
                cols_ref[kp, r] = beside(halves(old) - taken).reshape(4, 128, 256)
            return carry

        lax.fori_loop(0, p, subtract, 0)

        @pl.when((t >= 2) & (order(t - 2 + 2 * (1 - (t + 10) // 12)) < 8))
        def _():
            due = order(t - 2) + 4
            arrive(second(due))
            go(third(due))

        @pl.when(t < 3)
        def _():
            arrive(second(t + 1))
            go(third(t + 1))

        now = cols_ref[kp].reshape(2048, 256)
        block = invert_block(quarters(dot(now, now, TN)))

        @pl.when((t >= 1) & (order(t - 1 + (1 - (t + 11) // 12)) < 8))
        def _():
            due = order(t - 1) + 4
            arrive(first(due))
            go(second(due))

        high, low = split(block)
        weights = jnp.concatenate(
            [jnp.concatenate([high, high], axis=1), jnp.concatenate([low, low], axis=1)], axis=0)
        for r in range(4):
            rows = pl.ds(512 * r, 512)
            q_ref[kp, rows] = beside(halves(dot(cols_ref[kp, r].reshape(512, 256), weights, NT)))

        @pl.when(k < 2)
        def _():
            cols_ref[kp + 4, y, x, half] = beside(quarters(dot(pair_ref[...], q_ref[kp], NN)))
            go(first(kp + 4))

        @pl.when(k == 2)
        def _():
            rows = pl.ds(pl.multiple_of(head * 128, 128), 128)
            basis_ref[:, pl.ds(pl.multiple_of(p * 128, 128), 128)] = halves(q_ref[kp, rows].astype(F32))

        return carry

    lax.fori_loop(0, 12, task, 0)
    total = jnp.zeros((512, 256), F32)
    for block in range(16):
        kv = kv_ref[block // 4, block % 4]
        total = total + dot(kv, q_ref[8 + head // 4, 128 * block:128 * block + 128], NN)
    total = halves(total)
    for n in range(4):
        @pl.when(head % 4 == n)
        def _():
            latent_ref[...] = total[:, 32 * n:32 * n + 32]


def iterate(corr, sketch, kv):
    return pl.pallas_call(
        iterate_kernel,
        out_shape=(jax.ShapeDtypeStruct((128, 512), F32), jax.ShapeDtypeStruct((512, 32), F32)),
        in_specs=[VM] * 3, out_specs=(VM, VM),
        scratch_shapes=[
            pltpu.VMEM((12, 4, 4, 128, 256), BF16),
            pltpu.VMEM((12, 2048, 256), BF16),
            pltpu.VMEM((128, 2048), BF16),
            DMA((12, 13)),
            DMA((12, 13)),
        ],
        compiler_params=params(3),
    )(corr, sketch, kv)


def local(states, gain, kv_weight, kv_bias, sketch):
    kv, whole_sketch = make_kv(states, gain, kv_weight, kv_bias, sketch)
    return iterate(make_corr(kv), whole_sketch, kv)


def solution(mesh):
    in_specs = (P("dp", "head"), P("head"), P("head", None), P("head"), P("head", None))
    out_specs = (P("head", None), P("dp", "head"))
    return jax.shard_map(local, mesh=mesh, in_specs=in_specs, out_specs=out_specs, check_vma=False)
```

time: 300 us -> 230 us (0.77)
  Pallas kernels: 270 us -> 220 us
  between operations: 14.4 us -> 0.67 us
  local copies, waits for them, and re-layouts: 8.22 us -> 4.76 us
    pallas_call x9 -> x3, Pallas kernels: 270 us -> 220 us  [the longest x1 124 us: iterate(): pl.pallas_call(iterate_kernel, out_shape=(jax.ShapeDtypeStruct((128, 512)...]
    unnamed x12 -> x9, local copies, waits for them, and re-layouts: 7.49 us -> 4.02 us
  transfers between devices with their start and end apart: 1 -> 0, of which waited for: 0 -> 0; matrix products, arithmetic and copies ran while one was open for 0% -> 0% of each run, Pallas kernels for 34% -> 0%
where the time goes in v2:
time: 230 us; the launch traced here: 226 us
  Pallas kernels  220 us (96%)
  local copies, waits for them, and re-layouts  4.76 us (2%)
    pallas_call x1, Pallas kernels, iterate(): pl.pallas_call(iterate_kernel, out_shape=(jax.ShapeDtypeStruct((128, 512)...  124 us
    pallas_call x1, Pallas kernels, make_kv(): pl.pallas_call(kv_kernel, out_shape=(jax.ShapeDtypeStruct((4, 4, 512, 128...  58.9 us
    pallas_call x1, Pallas kernels, make_corr(): pl.pallas_call(corr_kernel, out_shape=jax.ShapeDtypeStruct((64, 2048), F3...  37.2 us

profile of v2, /device:TPU:1, one launch (start us, length us, event | category | flops | bytes accessed | tf_op | source)
XLA Modules:
  0.0 225.6 jit_solution(18198376741485132112)
XLA Ops:
  0.6 0.0 copy-start
  0.6 1.0 copy-done
  1.7 0.0 copy-start.1
  1.7 0.9 copy-done.1
  2.6 0.0 copy-start.2
  2.6 0.7 copy-done.2
  3.3 0.0 copy-start.3
  3.3 0.7 copy-done.3
  4.0 58.9 %shard_map.68 = (bf16[4,4,512,128]{3,2,1,0:T(8,128)(2,1)S(1)}, bf16[4,4,128,512]{3,2,1,0:T(8,128)(2,1)S(1)}) custom-call(bf16[512,512]{1,0:T(8,128)(2,1)S(1)} %copy-done, f32[1,512]{1,0:T(1,128)S(1)} %bitcast.2, bf16[512,2048]{1,0:T(8,128)(2,1)} %w_ref.1, f32[1,128]{1,0:T(1,128)S(1)} %bitcast.3, s32[128,512]{1,0:T(8,128)S(1)} %copy-done.1), custom_call_target="tpu_custom_call" | custom-call | tf_op jit(solution)/shard_map/pallas_call | solution.py:161
  62.9 37.2 %shard_map.69.g_ref = f32[64,2048]{1,0:T(8,128)S(1)} custom-call(bf16[4,4,512,128]{3,2,1,0:T(8,128)(2,1)S(1)} %get-tuple-element.4.kv_ref), custom_call_target="tpu_custom_call" | custom-call | tf_op jit(solution)/shard_map/pallas_call | solution.py:218
  100.1 124.0 %shard_map.70 = (f32[128,512]{1,0:T(8,128)S(1)}, f32[512,32]{1,0:T(8,128)S(1)}) custom-call(f32[64,2048]{1,0:T(8,128)S(1)} %shard_map.69.g_ref, bf16[4,4,128,512]{3,2,1,0:T(8,128)(2,1)S(1)} %get-tuple-element.5.s_ref, bf16[4,4,512,128]{3,2,1,0:T(8,128)(2,1)S(1)} %get-tuple-element.4.kv_ref), custom_call_target="tpu_custom_call" | custom-call | tf_op jit(solution)/shard_map/pallas_call | solution.py:411
  224.1 0.7 copy.7
  224.9 0.7 copy.9
Async XLA Ops:
  0.6 1.0 copy-start
  1.7 0.9 copy-start.1
  2.6 0.7 copy-start.2
  3.3 0.7 copy-start.3

commit v3 on v2

v3 whole, which is shorter than its diff:
```python
import jax
import jax.numpy as jnp
from jax import lax
from jax.experimental import pallas as pl
from jax.experimental.pallas import tpu as pltpu
from jax.sharding import PartitionSpec as P

D = 8192
F32 = jnp.float32
BF16 = jnp.bfloat16
MESH = pl.DeviceIdType.MESH
VM = pl.BlockSpec(memory_space=pltpu.VMEM)
DMA = pltpu.SemaphoreType.DMA


def position():
    dp, head = lax.axis_index("dp"), lax.axis_index("head")
    return dp, head, dp // 2, dp % 2, head // 4, head % 4


def greet(devices):
    barrier = pltpu.get_barrier_semaphore()
    for device in devices:
        pl.semaphore_signal(barrier, inc=1, device_id=device, device_id_type=MESH)
    pl.semaphore_wait(barrier, len(devices))


class Copies:
    def __init__(self, send_sem, recv_sem):
        self.send_sem, self.recv_sem, self.started = send_sem, recv_sem, []

    def go(self, src, dst, device):
        n = len(self.started)
        copy = pltpu.make_async_remote_copy(
            src_ref=src, dst_ref=dst, send_sem=self.send_sem.at[n],
            recv_sem=self.recv_sem.at[n], device_id=device, device_id_type=MESH,
        )
        copy.start()
        self.started.append(copy)
        return copy

    def finish(self):
        for copy in self.started:
            copy.wait_send()


def dot(a, b, dims, precision=None):
    return lax.dot_general(a, b, (dims, ((), ())), precision=precision, preferred_element_type=F32)


NN, NT, TN = ((1,), (0,)), ((1,), (1,)), ((0,), (0,))
HI = lax.Precision.HIGHEST


def split(v):
    high = v.astype(BF16)
    return high, (v - high.astype(F32)).astype(BF16)


def make_kv(place, copies, st_ref, gain_ref, w_any, bias_ref, kv_ref, w_ref, sq_ref, n_ref, part_ref, own_ref,
            recv_ref, recv2_ref, w_sem, meet):
    dp, head, _, _, y, x = place
    load = pltpu.make_async_copy(w_any, w_ref, w_sem)
    load.start()
    others = [lax.rem(head + k, 16) for k in range(1, 16)]
    xs = [lax.rem(x + k, 4) for k in (2, 1, 3)]
    ys = [lax.rem(y + k, 4) for k in (2, 1, 3)]
    to_x = [(dp, y * 4 + v) for v in xs]
    to_y = [(dp, v * 4 + x) for v in ys]

    values = st_ref[...].astype(F32)
    sq_ref[head] = dot(jnp.ones((8, 512), F32), values * values, NT, HI)
    meet()
    arrivals = [copies.go(sq_ref.at[head, 0:1], sq_ref.at[head, 0:1], (dp, v)) for v in others]
    for copy in arrivals:
        copy.wait_recv()
    total = sq_ref[0, 0:1]
    for k in range(1, 16):
        total = total + sq_ref[k, 0:1]
    scale = lax.rsqrt(total / D + 1e-06)
    column = jnp.transpose(jnp.broadcast_to(scale, (128, 512)))
    for block in range(4):
        cols = pl.ds(128 * block, 128)
        part = st_ref[:, cols].astype(F32) * column * gain_ref[:, cols]
        n_ref[:, cols] = part.astype(BF16)
    load.wait()

    def product(rows, owner):
        cols = pl.ds(pl.multiple_of(owner * 128, 128), 128)
        return dot(n_ref[rows], w_ref[:, cols], NN)

    chunks = [pl.ds(128 * n, 128) for n in range(4)]
    first = [[], [], [], []]
    for k in range(3):
        for v in range(4):
            part_ref[v, xs[k]] = product(pl.ds(0, 512), v * 4 + xs[k]).astype(BF16)
        for n in range(2):
            first[n].append(copies.go(part_ref.at[:, xs[k], chunks[n]], recv_ref.at[n, k], to_x[k]))
    for v in range(4):
        whole = product(pl.ds(0, 512), v * 4 + x)
        part_ref[v, x] = whole.astype(BF16)
        own_ref[0, v] = whole[:128]
        own_ref[1, v] = whole[128:256]
    for n in range(2, 4):
        for k in range(3):
            first[n].append(copies.go(part_ref.at[ys[k], :, chunks[n]], recv_ref.at[n, k], to_y[k]))
    for v in range(4):
        own = product(pl.ds(256, 256), y * 4 + v)
        own_ref[2, v] = own[:128]
        own_ref[3, v] = own[128:]
    sequence = (0, 2, 1, 3)
    second = [None] * 4
    for n in sequence:
        for copy in first[n]:
            copy.wait_recv()
        for v in range(4):
            own_ref[n, v] += (recv_ref[n, 0, v].astype(F32) + recv_ref[n, 1, v].astype(F32)) + recv_ref[
                n, 2, v].astype(F32)
        far, to = (ys, to_y) if n < 2 else (xs, to_x)
        second[n] = [copies.go(own_ref.at[n, far[k]], recv2_ref.at[n, k], to[k]) for k in range(3)]
    third = [None] * 4
    for n in sequence:
        for copy in second[n]:
            copy.wait_recv()
        summed = own_ref[n, y if n < 2 else x] + (recv2_ref[n, 0] + recv2_ref[n, 1]) + recv2_ref[n, 2]
        kv_ref[y, x, chunks[n]] = (summed + bias_ref[...]).astype(BF16)
        block = kv_ref.at[y, x, chunks[n]]
        third[n] = [copies.go(block, block, d) for d in (to_x if n < 2 else to_y)]
    fourth = []
    for n in sequence:
        for copy in third[n]:
            copy.wait_recv()
        line = kv_ref.at[y, :, chunks[n]] if n < 2 else kv_ref.at[:, x, chunks[n]]
        fourth += [copies.go(line, line, d) for d in (to_y if n < 2 else to_x)]
    for copy in fourth:
        copy.wait_recv()


def make_corr(place, copies, kv_ref, sketch_ref, whole_ref, part, recv_half, recv_z, g_ref):
    dp, head, z, c, y, x = place
    sibling = (dp + 1 - 2 * c, head)
    zs = [lax.rem(z + k, 8) for k in (4, 3, 5, 2, 6, 1, 7)]
    to_z = [(v * 2 + c, head) for v in zs]
    to_x = [(dp, y * 4 + lax.rem(x + k, 4)) for k in (1, 2, 3)]
    to_y = [(dp, lax.rem(y + k, 4) * 4 + x) for k in (1, 2, 3)]
    half = pl.ds(pl.multiple_of(c * 64, 64), 64)
    part_a = pl.ds(pl.multiple_of(c * 64, 32), 32)
    part_b = pl.ds(pl.multiple_of(c * 64 + 32, 32), 32)
    whole_ref[y, x, half] = sketch_ref[half].astype(BF16)
    spread_a = [copies.go(whole_ref.at[y, x, part_a], whole_ref.at[y, x, part_a], d) for d in to_x]
    spread_b = [copies.go(whole_ref.at[y, x, part_b], whole_ref.at[y, x, part_b], d) for d in to_y]
    mine = kv_ref[y, x]
    for owner in range(8):
        pair = jnp.concatenate([kv_ref[owner // 2, owner % 2 * 2], kv_ref[owner // 2, owner % 2 * 2 + 1]], axis=1)
        value = dot(mine, pair, TN)
        part[0, owner] = value[:64]
        part[1, owner] = value[64:]
    swaps = [copies.go(part.at[1 - c, v], recv_half.at[v], sibling) for v in zs + [z]]
    for copy in spread_a + spread_b:
        copy.wait_recv()
    spread = [copies.go(whole_ref.at[y, :, part_a], whole_ref.at[y, :, part_a], d) for d in to_y]
    spread += [copies.go(whole_ref.at[:, x, part_b], whole_ref.at[:, x, part_b], d) for d in to_x]
    first = []
    for k in range(7):
        swaps[k].wait_recv()
        part[c, zs[k]] += recv_half[zs[k]]
        first.append(copies.go(part.at[c, zs[k]], recv_z.at[k], to_z[k]))
    swaps[7].wait_recv()
    total = part[c, z] + recv_half[z]
    for k in range(7):
        first[k].wait_recv()
        total = total + recv_z[k]
    cols = pl.ds(pl.multiple_of(z * 256, 256), 256)
    g_ref[:, cols] = total
    second = [copies.go(g_ref.at[:, cols], g_ref.at[:, cols], d) for d in to_z]
    for copy in spread:
        copy.wait_recv()
    last = copies.go(whole_ref.at[:, :, half], whole_ref.at[:, :, half], sibling)
    for copy in second:
        copy.wait_recv()
    last.wait_recv()


def invert_block(a):
    shape = (8, 128)
    rows = [a[8 * g:8 * g + 8] for g in range(16)]
    lane = lax.broadcasted_iota(jnp.int32, shape, 1)
    sub = lax.broadcasted_iota(jnp.int32, shape, 0)
    inverse = [(lane == sub + 8 * g).astype(F32) for g in range(16)]
    for p in range(16):
        spread = [[jnp.broadcast_to(rows[g][:, 8 * p + c:8 * p + c + 1], shape) for g in range(p, 16)]
                  for c in range(8)]
        pivots = None
        for r in range(8):
            pivot = jnp.broadcast_to(spread[r][0][r:r + 1], shape)
            pivots = pivot if pivots is None else jnp.where(sub == r, pivot, pivots)
            recip = 1.0 / pivot
            row = jnp.broadcast_to(rows[p][r:r + 1], shape) * recip
            inverse_row = jnp.broadcast_to(inverse[p][r:r + 1], shape) * recip
            heads = {c: jnp.broadcast_to(spread[c][0][r:r + 1], shape) * recip for c in range(r + 1, 8)}
            for i in range(16 - p):
                if i == 0 and r == 7:
                    continue
                factor = spread[r][i]
                if i == 0:
                    factor = jnp.where(sub > r, factor, 0.0)
                for c in range(r + 1, 8):
                    spread[c][i] = spread[c][i] - factor * heads[c]
                rows[p + i] = rows[p + i] - factor * row
                inverse[p + i] = inverse[p + i] - factor * inverse_row
        inverse[p] = inverse[p] * lax.rsqrt(pivots)
    return jnp.concatenate(inverse, axis=0)


def order(t):
    r = t % 4
    return t + (r // 3) * (1 - t // 11) - (1 - (r + 3) // 4) * ((t + 11) // 12)


def beside(v):
    return jnp.concatenate(split(v), axis=1)


def halves(v):
    return v[:, :128] + v[:, 128:]


def quarters(v):
    rows = v.shape[0] // 2
    return halves(v[:rows]) + halves(v[rows:])


def iterate(place, g_ref, s_ref, kv_ref, basis_ref, latent_ref, cols_ref, q_ref, pair_ref, send_sem, recv_sem):
    dp, head, _, c, y, x = place
    xs = [lax.rem(x + k, 4) for k in (1, 2, 3)]
    ys = [lax.rem(y + k, 4) for k in (1, 2, 3)]
    to_x = [(dp, y * 4 + v) for v in xs]
    to_y = [(dp, v * 4 + x) for v in ys]
    sibling = (dp + 1 - 2 * c, head)
    half = pl.ds(pl.multiple_of(c * 64, 64), 64)
    part_a = pl.ds(pl.multiple_of(c * 64, 32), 32)
    part_b = pl.ds(pl.multiple_of(c * 64 + 32, 32), 32)

    def copy(kp, n, where, device):
        here = cols_ref.at[(kp,) + where]
        return pltpu.make_async_remote_copy(
            src_ref=here, dst_ref=here, send_sem=send_sem.at[kp, n], recv_sem=recv_sem.at[kp, n],
            device_id=device, device_id_type=MESH,
        )

    every = slice(None)

    def first(kp):
        return [copy(kp, n, (y, x, part_a), to_x[n]) for n in range(3)] + [
            copy(kp, 3 + n, (y, x, part_b), to_y[n]) for n in range(3)]

    def second(kp):
        return [copy(kp, 6 + n, (y, every, part_a), to_y[n]) for n in range(3)] + [
            copy(kp, 9 + n, (every, x, part_b), to_x[n]) for n in range(3)]

    def third(kp):
        return [copy(kp, 12, (every, every, half), sibling)]

    def go(some):
        for one in some:
            one.start()

    def arrive(some):
        for one in some:
            one.wait_recv()

    def leave(some):
        for one in some:
            one.wait_send()

    pair_ref[:64], pair_ref[64:] = split(g_ref[...])
    for p in range(4):
        s = s_ref[:, :, :, 128 * p:128 * p + 128].reshape(2048, 128)
        new = dot(pair_ref[...], s, NN)
        cols_ref[p, y, x, half] = beside(new[:64] + new[64:])
        go(first(p))
    for p in range(4):
        arrive(first(p))
        go(second(p))
    arrive(second(0))
    go(third(0))

    def task(t, carry):
        kp = order(t)
        k, p = kp // 4, kp % 4
        arrive(third(kp))
        leave(first(kp) + second(kp) + third(kp))

        for n in range(1, 4):
            @pl.when(p == n)
            def _():
                now = cols_ref[kp].reshape(2048, 256)
                factors = [beside(quarters(dot(q_ref[k * 4 + q], now, TN))) for q in range(n)]
                weights = [jnp.concatenate([factor, factor], axis=0) for factor in factors]
                taken = dot(q_ref[k * 4], weights[0], NN)
                for q in range(1, n):
                    taken = taken + dot(q_ref[k * 4 + q], weights[q], NN)
                cols_ref[kp] = beside(halves(now.astype(F32)) - halves(taken)).reshape(4, 4, 128, 256)

        @pl.when((t >= 2) & (order(t - 2 + 2 * (1 - (t + 10) // 12)) < 8))
        def _():
            due = order(t - 2) + 4
            arrive(second(due))
            go(third(due))

        @pl.when(t < 3)
        def _():
            arrive(second(t + 1))
            go(third(t + 1))

        now = cols_ref[kp].reshape(2048, 256)
        block = invert_block(quarters(dot(now, now, TN)))

        @pl.when((t >= 1) & (order(t - 1 + (1 - (t + 11) // 12)) < 8))
        def _():
            due = order(t - 1) + 4
            arrive(first(due))
            go(second(due))

        high, low = split(block)
        weights = jnp.concatenate(
            [jnp.concatenate([high, high], axis=1), jnp.concatenate([low, low], axis=1)], axis=0)
        for r in range(4):
            rows = pl.ds(512 * r, 512)
            q_ref[kp, rows] = beside(halves(dot(cols_ref[kp, r].reshape(512, 256), weights, NT)))

        @pl.when(k < 2)
        def _():
            cols_ref[kp + 4, y, x, half] = beside(quarters(dot(pair_ref[...], q_ref[kp], NN)))
            go(first(kp + 4))

        @pl.when(k == 2)
        def _():
            rows = pl.ds(pl.multiple_of(head * 128, 128), 128)
            basis_ref[:, pl.ds(pl.multiple_of(p * 128, 128), 128)] = halves(q_ref[kp, rows].astype(F32))

        return carry

    lax.fori_loop(0, 12, task, 0)
    total = jnp.zeros((512, 256), F32)
    for block in range(16):
        kv = kv_ref[block // 4, block % 4]
        total = total + dot(kv, q_ref[8 + head // 4, 128 * block:128 * block + 128], NN)
    total = halves(total)
    for n in range(4):
        @pl.when(head % 4 == n)
        def _():
            latent_ref[...] = total[:, 32 * n:32 * n + 32]


def kernel(st_ref, gain_ref, w_any, bias_ref, sketch_ref, basis_ref, latent_ref, kv_ref, w_ref, sq_ref, n_ref,
           part_ref, own_ref, recv_ref, recv2_ref, whole_ref, gpart_ref, half_ref, z_ref, g_ref, cols_ref, q_ref,
           pair_ref, w_sem, send_sem, recv_sem, panel_send, panel_recv):
    place = position()
    dp, head, z, c, _, _ = place
    copies = Copies(send_sem, recv_sem)

    def meet():
        greet([(dp, lax.rem(head + k, 16)) for k in range(1, 16)] + [(dp + 1 - 2 * c, head)] + [
            (lax.rem(z + k, 8) * 2 + c, head) for k in range(1, 8)])

    make_kv(place, copies, st_ref, gain_ref, w_any, bias_ref, kv_ref, w_ref, sq_ref, n_ref, part_ref, own_ref,
            recv_ref, recv2_ref, w_sem, meet)
    make_corr(place, copies, kv_ref, sketch_ref, whole_ref, gpart_ref, half_ref, z_ref, g_ref)
    iterate(place, g_ref, whole_ref, kv_ref, basis_ref, latent_ref, cols_ref, q_ref, pair_ref, panel_send, panel_recv)
    copies.finish()


def local(states, gain, kv_weight, kv_bias, sketch):
    n = 15 + 4 * 12 + 13 + 8 + 14
    return pl.pallas_call(
        kernel,
        out_shape=(jax.ShapeDtypeStruct((128, 512), F32), jax.ShapeDtypeStruct((512, 32), F32)),
        in_specs=[VM, VM, pl.BlockSpec(memory_space=pl.ANY), VM, VM],
        out_specs=(VM, VM),
        scratch_shapes=[
            pltpu.VMEM((4, 4, 512, 128), BF16),
            pltpu.VMEM((512, 2048), BF16),
            pltpu.VMEM((16, 8, 512), F32),
            pltpu.VMEM((512, 512), BF16),
            pltpu.VMEM((4, 4, 512, 128), BF16),
            pltpu.VMEM((4, 4, 128, 128), F32),
            pltpu.VMEM((4, 3, 4, 128, 128), BF16),
            pltpu.VMEM((4, 3, 128, 128), F32),
            pltpu.VMEM((4, 4, 128, 512), BF16),
            pltpu.VMEM((2, 8, 64, 256), F32),
            pltpu.VMEM((8, 64, 256), F32),
            pltpu.VMEM((7, 64, 256), F32),
            pltpu.VMEM((64, 2048), F32),
            pltpu.VMEM((12, 4, 4, 128, 256), BF16),
            pltpu.VMEM((12, 2048, 256), BF16),
            pltpu.VMEM((128, 2048), BF16),
            DMA,
            DMA((n,)),
            DMA((n,)),
            DMA((12, 13)),
            DMA((12, 13)),
        ],
        compiler_params=pltpu.CompilerParams(collective_id=1, has_side_effects=True, vmem_limit_bytes=60 << 20),
    )(states, gain.reshape(1, 512), kv_weight, kv_bias.reshape(1, 128), sketch)


def solution(mesh):
    in_specs = (P("dp", "head"), P("head"), P("head", None), P("head"), P("head", None))
    out_specs = (P("head", None), P("dp", "head"))
    return jax.shard_map(local, mesh=mesh, in_specs=in_specs, out_specs=out_specs, check_vma=False)
```

time: 230 us -> 209 us (0.909); the launches traced: 226 us -> 207 us
  Pallas kernels: 220 us -> 203 us
    pallas_call x3 -> x1, Pallas kernels: 220 us -> 203 us  [local(): pl.pallas_call(kernel, out_shape=(jax.ShapeDtypeStruct((128, 512), F32),...]
    unnamed x9 -> x1, local copies, waits for them, and re-layouts: 4.02 us -> 1.67 us
where the time goes in v3:
time: 209 us; the launch traced here: 207 us
  Pallas kernels  203 us (97%)
  local copies, waits for them, and re-layouts  3.36 us (2%)
    pallas_call x1, Pallas kernels, local(): pl.pallas_call(kernel, out_shape=(jax.ShapeDtypeStruct((128, 512), F32),...  203 us

profile of v3, /device:TPU:1, one launch (start us, length us, event | category | flops | bytes accessed | tf_op | source)
XLA Modules:
  0.0 207.3 jit_solution(13549591270454918769)
XLA Ops:
  0.6 203.3 %shard_map.68 = (f32[128,512]{1,0:T(8,128)}, f32[512,32]{1,0:T(8,128)}) custom-call(bf16[512,512]{1,0:T(8,128)(2,1)} %st_ref.1, f32[1,512]{1,0:T(1,128)} %bitcast.2, bf16[512,2048]{1,0:T(8,128)(2,1)} %w_any.1, f32[1,128]{1,0:T(1,128)} %bitcast.3, s32[128,512]{1,0:T(8,128)} %sketch_ref.1), custom_call_target="tpu_custom_call" | custom-call | tf_op jit(solution)/shard_map/pallas_call | solution.py:376
  204.0 1.7 copy.7
  205.7 1.7 copy.9

commit v4 on v3

--- a/solution.py
+++ b/solution.py
@@ -57,9 +57,13 @@
     return high, (v - high.astype(F32)).astype(BF16)
 
 
-def make_kv(place, copies, st_ref, gain_ref, w_any, bias_ref, kv_ref, w_ref, sq_ref, n_ref, part_ref, own_ref,
-            recv_ref, recv2_ref, w_sem, meet):
-    dp, head, _, _, y, x = place
+def make_kv(place, copies, st_ref, gain_ref, w_any, bias_ref, sketch_ref, kv_ref, w_ref, sq_ref, n_ref, part_ref,
+            own_ref, recv_ref, recv2_ref, whole_ref, w_sem, meet):
+    dp, head, _, c, y, x = place
+    half = pl.ds(pl.multiple_of(c * 64, 64), 64)
+    part_a = pl.ds(pl.multiple_of(c * 64, 32), 32)
+    part_b = pl.ds(pl.multiple_of(c * 64 + 32, 32), 32)
+    whole_ref[y, x, half] = sketch_ref[half].astype(BF16)
     load = pltpu.make_async_copy(w_any, w_ref, w_sem)
     load.start()
     others = [lax.rem(head + k, 16) for k in range(1, 16)]
@@ -69,9 +73,13 @@
     to_y = [(dp, v * 4 + x) for v in ys]
 
     values = st_ref[...].astype(F32)
-    sq_ref[head] = dot(jnp.ones((8, 512), F32), values * values, NT, HI)
+    high, low = split(values * values)
+    ones = jnp.ones((16, 512), BF16)
+    sq_ref[head] = (dot(ones, high, NT) + dot(ones, low, NT))[:8]
     meet()
     arrivals = [copies.go(sq_ref.at[head, 0:1], sq_ref.at[head, 0:1], (dp, v)) for v in others]
+    spread = [copies.go(whole_ref.at[y, x, part_a], whole_ref.at[y, x, part_a], d) for d in to_x]
+    spread += [copies.go(whole_ref.at[y, x, part_b], whole_ref.at[y, x, part_b], d) for d in to_y]
     for copy in arrivals:
         copy.wait_recv()
     total = sq_ref[0, 0:1]
@@ -89,6 +97,10 @@
         cols = pl.ds(pl.multiple_of(owner * 128, 128), 128)
         return dot(n_ref[rows], w_ref[:, cols], NN)
 
+    for copy in spread:
+        copy.wait_recv()
+    spread = [copies.go(whole_ref.at[y, :, part_a], whole_ref.at[y, :, part_a], d) for d in to_y]
+    spread += [copies.go(whole_ref.at[:, x, part_b], whole_ref.at[:, x, part_b], d) for d in to_x]
     chunks = [pl.ds(128 * n, 128) for n in range(4)]
     first = [[], [], [], []]
     for k in range(3):
@@ -118,6 +130,9 @@
                 n, 2, v].astype(F32)
         far, to = (ys, to_y) if n < 2 else (xs, to_x)
         second[n] = [copies.go(own_ref.at[n, far[k]], recv2_ref.at[n, k], to[k]) for k in range(3)]
+    for copy in spread:
+        copy.wait_recv()
+    spread = copies.go(whole_ref.at[:, :, half], whole_ref.at[:, :, half], (dp + 1 - 2 * c, head))
     third = [None] * 4
     for n in sequence:
         for copy in second[n]:
@@ -132,53 +147,81 @@
             copy.wait_recv()
         line = kv_ref.at[y, :, chunks[n]] if n < 2 else kv_ref.at[:, x, chunks[n]]
         fourth += [copies.go(line, line, d) for d in (to_y if n < 2 else to_x)]
-    for copy in fourth:
+    for copy in fourth + [spread]:
         copy.wait_recv()
 
 
-def make_corr(place, copies, kv_ref, sketch_ref, whole_ref, part, recv_half, recv_z, g_ref):
+class Corr:
+    def __init__(self, place, copies, kv_ref, part, recv_half, recv_z, g_ref):
+        dp, head, z, c, y, x = place
+        self.copies, self.z, self.c = copies, z, c
+        self.part, self.recv_half, self.recv_z, self.g_ref = part, recv_half, recv_z, g_ref
+        self.sibling = (dp + 1 - 2 * c, head)
+        self.zs = [lax.rem(z + k, 8) for k in (4, 3, 5, 2, 6, 1, 7)]
+        self.to_z = [(v * 2 + c, head) for v in self.zs]
+
+    def terms(self, kv_ref, mine):
+        for owner in range(8):
+            pair = [kv_ref[owner // 2, owner % 2 * 2 + n] for n in range(2)]
+            value = dot(mine, jnp.concatenate(pair, axis=1), TN)
+            self.part[0, owner] = value[:64]
+            self.part[1, owner] = value[64:]
+        self.swaps = [
+            self.copies.go(self.part.at[1 - self.c, v], self.recv_half.at[v], self.sibling) for v in self.zs + [self.z]]
+
+    def swapped(self):
+        self.first = []
+        for k in range(7):
+            v = self.zs[k]
+            self.swaps[k].wait_recv()
+            self.part[self.c, v] += self.recv_half[v]
+            self.first.append(self.copies.go(self.part.at[self.c, v], self.recv_z.at[k], self.to_z[k]))
+        self.swaps[7].wait_recv()
+
+    def summed(self):
+        total = self.part[self.c, self.z] + self.recv_half[self.z]
+        for k in range(7):
+            self.first[k].wait_recv()
+            total = total + self.recv_z[k]
+        cols = pl.ds(pl.multiple_of(self.z * 256, 256), 256)
+        self.g_ref[:, cols] = total
+        self.second = [self.copies.go(self.g_ref.at[:, cols], self.g_ref.at[:, cols], d) for d in self.to_z]
+
+    def gathered(self):
+        for copy in self.second:
+            copy.wait_recv()
+
+
+def first_columns(place, copies, corr, kv_ref, whole_ref, cpart_ref, chalf_ref, cz_ref, c0_ref):
     dp, head, z, c, y, x = place
-    sibling = (dp + 1 - 2 * c, head)
-    zs = [lax.rem(z + k, 8) for k in (4, 3, 5, 2, 6, 1, 7)]
-    to_z = [(v * 2 + c, head) for v in zs]
-    to_x = [(dp, y * 4 + lax.rem(x + k, 4)) for k in (1, 2, 3)]
-    to_y = [(dp, lax.rem(y + k, 4) * 4 + x) for k in (1, 2, 3)]
-    half = pl.ds(pl.multiple_of(c * 64, 64), 64)
-    part_a = pl.ds(pl.multiple_of(c * 64, 32), 32)
-    part_b = pl.ds(pl.multiple_of(c * 64 + 32, 32), 32)
-    whole_ref[y, x, half] = sketch_ref[half].astype(BF16)
-    spread_a = [copies.go(whole_ref.at[y, x, part_a], whole_ref.at[y, x, part_a], d) for d in to_x]
-    spread_b = [copies.go(whole_ref.at[y, x, part_b], whole_ref.at[y, x, part_b], d) for d in to_y]
     mine = kv_ref[y, x]
+    products = jnp.zeros((512, 512), F32)
     for owner in range(8):
-        pair = jnp.concatenate([kv_ref[owner // 2, owner % 2 * 2], kv_ref[owner // 2, owner % 2 * 2 + 1]], axis=1)
-        value = dot(mine, pair, TN)
-        part[0, owner] = value[:64]
-        part[1, owner] = value[64:]
-    swaps = [copies.go(part.at[1 - c, v], recv_half.at[v], sibling) for v in zs + [z]]
-    for copy in spread_a + spread_b:
-        copy.wait_recv()
-    spread = [copies.go(whole_ref.at[y, :, part_a], whole_ref.at[y, :, part_a], d) for d in to_y]
-    spread += [copies.go(whole_ref.at[:, x, part_b], whole_ref.at[:, x, part_b], d) for d in to_x]
-    first = []
-    for k in range(7):
-        swaps[k].wait_recv()
-        part[c, zs[k]] += recv_half[zs[k]]
-        first.append(copies.go(part.at[c, zs[k]], recv_z.at[k], to_z[k]))
-    swaps[7].wait_recv()
-    total = part[c, z] + recv_half[z]
+        pair = [kv_ref[owner // 2, owner % 2 * 2 + n] for n in range(2)]
+        there = [whole_ref[owner // 2, owner % 2 * 2 + n] for n in range(2)]
+        products = products + dot(jnp.concatenate(pair, axis=1), jnp.concatenate(there, axis=0), NN)
+    high, low = split(products)
+    value = dot(mine, high, TN) + dot(mine, low, TN)
+    cpart_ref[0] = value[:64]
+    cpart_ref[1] = value[64:]
+    swap = copies.go(cpart_ref.at[1 - c], chalf_ref, corr.sibling)
+    corr.terms(kv_ref, mine)
+    swap.wait_recv()
+    cpart_ref[c] += chalf_ref[...]
+
+    def rows(owner):
+        return pl.ds(pl.multiple_of(owner * 8, 8), 8)
+
+    first = [copies.go(cpart_ref.at[c, rows(corr.zs[k])], cz_ref.at[k], corr.to_z[k]) for k in range(7)]
+    total = cpart_ref[c, rows(z)]
     for k in range(7):
         first[k].wait_recv()
-        total = total + recv_z[k]
-    cols = pl.ds(pl.multiple_of(z * 256, 256), 256)
-    g_ref[:, cols] = total
-    second = [copies.go(g_ref.at[:, cols], g_ref.at[:, cols], d) for d in to_z]
-    for copy in spread:
-        copy.wait_recv()
-    last = copies.go(whole_ref.at[:, :, half], whole_ref.at[:, :, half], sibling)
+        total = total + cz_ref[k]
+    c0_ref[rows(z)] = total
+    second = [copies.go(c0_ref.at[rows(z)], c0_ref.at[rows(z)], d) for d in corr.to_z]
+    corr.swapped()
     for copy in second:
         copy.wait_recv()
-    last.wait_recv()
 
 
 def invert_block(a):
@@ -230,7 +273,8 @@
     return halves(v[:rows]) + halves(v[rows:])
 
 
-def iterate(place, g_ref, s_ref, kv_ref, basis_ref, latent_ref, cols_ref, q_ref, pair_ref, send_sem, recv_sem):
+def iterate(place, corr, c0_ref, kv_ref, basis_ref, latent_ref, cols_ref, q_ref, pair_ref, total_ref, send_sem,
+            recv_sem):
     dp, head, _, c, y, x = place
     xs = [lax.rem(x + k, 4) for k in (1, 2, 3)]
     ys = [lax.rem(y + k, 4) for k in (1, 2, 3)]
@@ -273,17 +317,15 @@
         for one in some:
             one.wait_send()
 
-    pair_ref[:64], pair_ref[64:] = split(g_ref[...])
     for p in range(4):
-        s = s_ref[:, :, :, 128 * p:128 * p + 128].reshape(2048, 128)
-        new = dot(pair_ref[...], s, NN)
-        cols_ref[p, y, x, half] = beside(new[:64] + new[64:])
+        cols_ref[p, y, x, half] = beside(c0_ref[:, 128 * p:128 * p + 128])
         go(first(p))
     for p in range(4):
         arrive(first(p))
         go(second(p))
     arrive(second(0))
     go(third(0))
+    corr.summed()
 
     def task(t, carry):
         kp = order(t)
@@ -302,19 +344,19 @@
                     taken = taken + dot(q_ref[k * 4 + q], weights[q], NN)
                 cols_ref[kp] = beside(halves(now.astype(F32)) - halves(taken)).reshape(4, 4, 128, 256)
 
+        @pl.when(t < 3)
+        def _():
+            arrive(second(t + 1))
+            go(third(t + 1))
+
+        now = cols_ref[kp].reshape(2048, 256)
+        block = invert_block(quarters(dot(now, now, TN)))
+
         @pl.when((t >= 2) & (order(t - 2 + 2 * (1 - (t + 10) // 12)) < 8))
         def _():
             due = order(t - 2) + 4
             arrive(second(due))
             go(third(due))
-
-        @pl.when(t < 3)
-        def _():
-            arrive(second(t + 1))
-            go(third(t + 1))
-
-        now = cols_ref[kp].reshape(2048, 256)
-        block = invert_block(quarters(dot(now, now, TN)))
 
         @pl.when((t >= 1) & (order(t - 1 + (1 - (t + 11) // 12)) < 8))
         def _():
@@ -329,6 +371,11 @@
             rows = pl.ds(512 * r, 512)
             q_ref[kp, rows] = beside(halves(dot(cols_ref[kp, r].reshape(512, 256), weights, NT)))
 
+        @pl.when(t == 0)
+        def _():
+            corr.gathered()
+            pair_ref[:64], pair_ref[64:] = split(corr.g_ref[...])
+
         @pl.when(k < 2)
         def _():
             cols_ref[kp + 4, y, x, half] = beside(quarters(dot(pair_ref[...], q_ref[kp], NN)))
@@ -343,19 +390,17 @@
 
     lax.fori_loop(0, 12, task, 0)
     total = jnp.zeros((512, 256), F32)
-    for block in range(16):
-        kv = kv_ref[block // 4, block % 4]
-        total = total + dot(kv, q_ref[8 + head // 4, 128 * block:128 * block + 128], NN)
-    total = halves(total)
-    for n in range(4):
-        @pl.when(head % 4 == n)
-        def _():
-            latent_ref[...] = total[:, 32 * n:32 * n + 32]
+    for owner in range(8):
+        pair = [kv_ref[owner // 2, owner % 2 * 2 + n] for n in range(2)]
+        there = q_ref[8 + head // 4, 256 * owner:256 * owner + 256]
+        total = total + dot(jnp.concatenate(pair, axis=1), there, NN)
+    total_ref[...] = jnp.transpose(halves(total))
+    latent_ref[...] = total_ref[pl.ds(pl.multiple_of(head % 4 * 32, 32), 32), :]
 
 
 def kernel(st_ref, gain_ref, w_any, bias_ref, sketch_ref, basis_ref, latent_ref, kv_ref, w_ref, sq_ref, n_ref,
-           part_ref, own_ref, recv_ref, recv2_ref, whole_ref, gpart_ref, half_ref, z_ref, g_ref, cols_ref, q_ref,
-           pair_ref, w_sem, send_sem, recv_sem, panel_send, panel_recv):
+           part_ref, own_ref, recv_ref, recv2_ref, whole_ref, gpart_ref, half_ref, z_ref, g_ref, cpart_ref, chalf_ref,
+           cz_ref, c0_ref, cols_ref, q_ref, pair_ref, total_ref, w_sem, send_sem, recv_sem, panel_send, panel_recv):
     place = position()
     dp, head, z, c, _, _ = place
     copies = Copies(send_sem, recv_sem)
@@ -364,18 +409,26 @@
         greet([(dp, lax.rem(head + k, 16)) for k in range(1, 16)] + [(dp + 1 - 2 * c, head)] + [
             (lax.rem(z + k, 8) * 2 + c, head) for k in range(1, 8)])
 
-    make_kv(place, copies, st_ref, gain_ref, w_any, bias_ref, kv_ref, w_ref, sq_ref, n_ref, part_ref, own_ref,
-            recv_ref, recv2_ref, w_sem, meet)
-    make_corr(place, copies, kv_ref, sketch_ref, whole_ref, gpart_ref, half_ref, z_ref, g_ref)
-    iterate(place, g_ref, whole_ref, kv_ref, basis_ref, latent_ref, cols_ref, q_ref, pair_ref, panel_send, panel_recv)
+    make_kv(place, copies, st_ref, gain_ref, w_any, bias_ref, sketch_ref, kv_ref, w_ref, sq_ref, n_ref, part_ref,
+            own_ref, recv_ref, recv2_ref, whole_ref, w_sem, meet)
+    corr = Corr(place, copies, kv_ref, gpart_ref, half_ref, z_ref, g_ref)
+    first_columns(place, copies, corr, kv_ref, whole_ref, cpart_ref, chalf_ref, cz_ref, c0_ref)
+    iterate(place, corr, c0_ref, kv_ref, basis_ref, latent_ref, cols_ref, q_ref, pair_ref, total_ref, panel_send,
+            panel_recv)
     copies.finish()
 
 
+def finish_kernel(basis_ref, latent_ref, basis_out, latent_out):
+    basis_out[...] = basis_ref[...]
+    latent_out[...] = latent_ref[...]
+
+
 def local(states, gain, kv_weight, kv_bias, sketch):
-    n = 15 + 4 * 12 + 13 + 8 + 14
-    return pl.pallas_call(
+    n = 15 + 4 * 12 + 13 + 8 + 14 + 15
+    shapes = (jax.ShapeDtypeStruct((128, 512), F32), jax.ShapeDtypeStruct((32, 512), F32))
+    basis, latent = pl.pallas_call(
         kernel,
-        out_shape=(jax.ShapeDtypeStruct((128, 512), F32), jax.ShapeDtypeStruct((512, 32), F32)),
+        out_shape=shapes,
         in_specs=[VM, VM, pl.BlockSpec(memory_space=pl.ANY), VM, VM],
         out_specs=(VM, VM),
         scratch_shapes=[
@@ -392,9 +445,14 @@
             pltpu.VMEM((8, 64, 256), F32),
             pltpu.VMEM((7, 64, 256), F32),
             pltpu.VMEM((64, 2048), F32),
+            pltpu.VMEM((2, 64, 512), F32),
+            pltpu.VMEM((64, 512), F32),
+            pltpu.VMEM((7, 8, 512), F32),
+            pltpu.VMEM((64, 512), F32),
             pltpu.VMEM((12, 4, 4, 128, 256), BF16),
             pltpu.VMEM((12, 2048, 256), BF16),
             pltpu.VMEM((128, 2048), BF16),
+            pltpu.VMEM((128, 512), F32),
             DMA,
             DMA((n,)),
             DMA((n,)),
@@ -403,6 +461,8 @@
         ],
         compiler_params=pltpu.CompilerParams(collective_id=1, has_side_effects=True, vmem_limit_bytes=60 << 20),
     )(states, gain.reshape(1, 512), kv_weight, kv_bias.reshape(1, 128), sketch)
+    basis, latent = pl.pallas_call(finish_kernel, out_shape=shapes, in_specs=[VM] * 2, out_specs=(VM, VM))(basis, latent)
+    return basis, latent.T
 
 
 def solution(mesh):

time: 209 us -> 184 us (0.88)
  Pallas kernels: 203 us -> 183 us
  local copies, waits for them, and re-layouts: 3.36 us -> 0 us
    pallas_call x1 -> x2, Pallas kernels: 203 us -> 183 us  [the longest x1 181 us: local(): pl.pallas_call(kernel, out_shape=shapes, in_specs=[VM, VM, pl.BlockSpec(m...]
where the time goes in v4:
time: 184 us
  Pallas kernels  183 us (99%)
    pallas_call x1, Pallas kernels, local(): pl.pallas_call(kernel, out_shape=shapes, in_specs=[VM, VM, pl.BlockSpec(m...  181 us

profile of v4, /device:TPU:1, one launch (start us, length us, event | category | flops | bytes accessed | tf_op | source)
XLA Modules:
  0.0 183.7 jit_solution(15398184493136956654)
XLA Ops:
  0.6 181.4 %shard_map.68 = (f32[128,512]{1,0:T(8,128)}, f32[32,512]{1,0:T(8,128)}) custom-call(bf16[512,512]{1,0:T(8,128)(2,1)} %st_ref.1, f32[1,512]{1,0:T(1,128)} %bitcast.3, bf16[512,2048]{1,0:T(8,128)(2,1)} %w_any.1, f32[1,128]{1,0:T(1,128)} %bitcast.4, s32[128,512]{1,0:T(8,128)} %sketch_ref.1), custom_call_target="tpu_custom_call" | custom-call | tf_op jit(solution)/shard_map/pallas_call | solution.py:429
  182.0 1.7 shard_map.69

commit v5 on v4

--- a/solution.py
+++ b/solution.py
@@ -75,18 +75,23 @@
     values = st_ref[...].astype(F32)
     high, low = split(values * values)
     ones = jnp.ones((16, 512), BF16)
-    sq_ref[head] = (dot(ones, high, NT) + dot(ones, low, NT))[:8]
+    squares = dot(ones, high, NT) + dot(ones, low, NT)
+    for n in range(4):
+        line = squares[0:8, 128 * n:128 * n + 128]
+        tile = line if n == 0 else jnp.where(lax.broadcasted_iota(jnp.int32, (8, 128), 0) == n, line, tile)
+    sq_ref[head] = tile
     meet()
-    arrivals = [copies.go(sq_ref.at[head, 0:1], sq_ref.at[head, 0:1], (dp, v)) for v in others]
+    arrivals = [copies.go(sq_ref.at[head], sq_ref.at[head], (dp, v)) for v in others]
     spread = [copies.go(whole_ref.at[y, x, part_a], whole_ref.at[y, x, part_a], d) for d in to_x]
     spread += [copies.go(whole_ref.at[y, x, part_b], whole_ref.at[y, x, part_b], d) for d in to_y]
     for copy in arrivals:
         copy.wait_recv()
-    total = sq_ref[0, 0:1]
+    total = sq_ref[0]
     for k in range(1, 16):
-        total = total + sq_ref[k, 0:1]
+        total = total + sq_ref[k]
     scale = lax.rsqrt(total / D + 1e-06)
-    column = jnp.transpose(jnp.broadcast_to(scale, (128, 512)))
+    column = jnp.concatenate(
+        [jnp.transpose(jnp.broadcast_to(scale[n:n + 1], (128, 128))) for n in range(4)], axis=0)
     for block in range(4):
         cols = pl.ds(128 * block, 128)
         part = st_ref[:, cols].astype(F32) * column * gain_ref[:, cols]
@@ -141,14 +146,14 @@
         kv_ref[y, x, chunks[n]] = (summed + bias_ref[...]).astype(BF16)
         block = kv_ref.at[y, x, chunks[n]]
         third[n] = [copies.go(block, block, d) for d in (to_x if n < 2 else to_y)]
-    fourth = []
+    fourth = [None] * 4
     for n in sequence:
         for copy in third[n]:
             copy.wait_recv()
         line = kv_ref.at[y, :, chunks[n]] if n < 2 else kv_ref.at[:, x, chunks[n]]
-        fourth += [copies.go(line, line, d) for d in (to_y if n < 2 else to_x)]
-    for copy in fourth + [spread]:
-        copy.wait_recv()
+        fourth[n] = [copies.go(line, line, d) for d in (to_y if n < 2 else to_x)]
+    spread.wait_recv()
+    return sequence, fourth
 
 
 class Corr:
@@ -192,20 +197,24 @@
             copy.wait_recv()
 
 
-def first_columns(place, copies, corr, kv_ref, whole_ref, cpart_ref, chalf_ref, cz_ref, c0_ref):
+def first_columns(place, copies, corr, sequence, arrivals, kv_ref, whole_ref, cpart_ref, chalf_ref, cz_ref, c0_ref):
     dp, head, z, c, y, x = place
-    mine = kv_ref[y, x]
-    products = jnp.zeros((512, 512), F32)
-    for owner in range(8):
-        pair = [kv_ref[owner // 2, owner % 2 * 2 + n] for n in range(2)]
-        there = [whole_ref[owner // 2, owner % 2 * 2 + n] for n in range(2)]
-        products = products + dot(jnp.concatenate(pair, axis=1), jnp.concatenate(there, axis=0), NN)
-    high, low = split(products)
-    value = dot(mine, high, TN) + dot(mine, low, TN)
+    value = jnp.zeros((128, 512), F32)
+    for n in sequence:
+        for copy in arrivals[n]:
+            copy.wait_recv()
+        rows = pl.ds(128 * n, 128)
+        products = jnp.zeros((128, 512), F32)
+        for owner in range(8):
+            pair = [kv_ref[owner // 2, owner % 2 * 2 + n, rows] for n in range(2)]
+            there = [whole_ref[owner // 2, owner % 2 * 2 + n] for n in range(2)]
+            products = products + dot(jnp.concatenate(pair, axis=1), jnp.concatenate(there, axis=0), NN)
+        high, low = split(products)
+        here = kv_ref[y, x, rows]
+        value = value + (dot(here, high, TN) + dot(here, low, TN))
     cpart_ref[0] = value[:64]
     cpart_ref[1] = value[64:]
     swap = copies.go(cpart_ref.at[1 - c], chalf_ref, corr.sibling)
-    corr.terms(kv_ref, mine)
     swap.wait_recv()
     cpart_ref[c] += chalf_ref[...]
 
@@ -213,6 +222,7 @@
         return pl.ds(pl.multiple_of(owner * 8, 8), 8)
 
     first = [copies.go(cpart_ref.at[c, rows(corr.zs[k])], cz_ref.at[k], corr.to_z[k]) for k in range(7)]
+    corr.terms(kv_ref, kv_ref[y, x])
     total = cpart_ref[c, rows(z)]
     for k in range(7):
         first[k].wait_recv()
@@ -256,8 +266,7 @@
 
 
 def order(t):
-    r = t % 4
-    return t + (r // 3) * (1 - t // 11) - (1 - (r + 3) // 4) * ((t + 11) // 12)
+    return t + (t // 7) * (1 - t // 8) - (t // 8) * (1 - t // 9)
 
 
 def beside(v):
@@ -352,17 +361,27 @@
         now = cols_ref[kp].reshape(2048, 256)
         block = invert_block(quarters(dot(now, now, TN)))
 
-        @pl.when((t >= 2) & (order(t - 2 + 2 * (1 - (t + 10) // 12)) < 8))
+        @pl.when((t >= 3) & (order(t - 2 + 2 * (1 - (t + 10) // 12)) < 8))
         def _():
             due = order(t - 2) + 4
             arrive(second(due))
             go(third(due))
 
-        @pl.when((t >= 1) & (order(t - 1 + (1 - (t + 11) // 12)) < 8))
+        @pl.when(t == 3)
+        def _():
+            arrive(second(4))
+            go(third(4))
+
+        @pl.when((t >= 2) & (order(t - 1 + (1 - (t + 11) // 12)) < 8))
         def _():
             due = order(t - 1) + 4
             arrive(first(due))
             go(second(due))
+
+        @pl.when(t == 2)
+        def _():
+            arrive(first(4))
+            go(second(4))
 
         high, low = split(block)
         weights = jnp.concatenate(
@@ -371,12 +390,14 @@
             rows = pl.ds(512 * r, 512)
             q_ref[kp, rows] = beside(halves(dot(cols_ref[kp, r].reshape(512, 256), weights, NT)))
 
-        @pl.when(t == 0)
+        @pl.when(t == 1)
         def _():
             corr.gathered()
             pair_ref[:64], pair_ref[64:] = split(corr.g_ref[...])
-
-        @pl.when(k < 2)
+            cols_ref[4, y, x, half] = beside(quarters(dot(pair_ref[...], q_ref[0], NN)))
+            go(first(4))
+
+        @pl.when((t > 0) & (k < 2))
         def _():
             cols_ref[kp + 4, y, x, half] = beside(quarters(dot(pair_ref[...], q_ref[kp], NN)))
             go(first(kp + 4))
@@ -409,10 +430,10 @@
         greet([(dp, lax.rem(head + k, 16)) for k in range(1, 16)] + [(dp + 1 - 2 * c, head)] + [
             (lax.rem(z + k, 8) * 2 + c, head) for k in range(1, 8)])
 
-    make_kv(place, copies, st_ref, gain_ref, w_any, bias_ref, sketch_ref, kv_ref, w_ref, sq_ref, n_ref, part_ref,
+    pending = make_kv(place, copies, st_ref, gain_ref, w_any, bias_ref, sketch_ref, kv_ref, w_ref, sq_ref, n_ref, part_ref,
             own_ref, recv_ref, recv2_ref, whole_ref, w_sem, meet)
     corr = Corr(place, copies, kv_ref, gpart_ref, half_ref, z_ref, g_ref)
-    first_columns(place, copies, corr, kv_ref, whole_ref, cpart_ref, chalf_ref, cz_ref, c0_ref)
+    first_columns(place, copies, corr, *pending, kv_ref, whole_ref, cpart_ref, chalf_ref, cz_ref, c0_ref)
     iterate(place, corr, c0_ref, kv_ref, basis_ref, latent_ref, cols_ref, q_ref, pair_ref, total_ref, panel_send,
             panel_recv)
     copies.finish()
@@ -434,7 +455,7 @@
         scratch_shapes=[
             pltpu.VMEM((4, 4, 512, 128), BF16),
             pltpu.VMEM((512, 2048), BF16),
-            pltpu.VMEM((16, 8, 512), F32),
+            pltpu.VMEM((16, 8, 128), F32),
             pltpu.VMEM((512, 512), BF16),
             pltpu.VMEM((4, 4, 512, 128), BF16),
             pltpu.VMEM((4, 4, 128, 128), F32),

time: 184 us -> 181 us (0.984); the launches traced: 184 us -> 178 us
  Pallas kernels: 183 us -> 178 us
    pallas_call x1, Pallas kernels: 181 us -> 176 us  [local(): pl.pallas_call(kernel, out_shape=shapes, in_specs=[VM, VM, pl.BlockSpec(m...]
where the time goes in v5:
time: 181 us; the launch traced here: 178 us
  Pallas kernels  178 us (98%)
    pallas_call x1, Pallas kernels, local(): pl.pallas_call(kernel, out_shape=shapes, in_specs=[VM, VM, pl.BlockSpec(m...  176 us

profile of v5, /device:TPU:1, one launch (start us, length us, event | category | flops | bytes accessed | tf_op | source)
XLA Modules:
  0.0 178.4 jit_solution(14725233119918262851)
XLA Ops:
  0.6 176.1 %shard_map.68 = (f32[128,512]{1,0:T(8,128)}, f32[32,512]{1,0:T(8,128)}) custom-call(bf16[512,512]{1,0:T(8,128)(2,1)} %st_ref.1, f32[1,512]{1,0:T(1,128)} %bitcast.3, bf16[512,2048]{1,0:T(8,128)(2,1)} %w_any.1, f32[1,128]{1,0:T(1,128)} %bitcast.4, s32[128,512]{1,0:T(8,128)} %sketch_ref.1), custom_call_target="tpu_custom_call" | custom-call | tf_op jit(solution)/shard_map/pallas_call | solution.py:450
  176.8 1.7 shard_map.69

commit v6 on v5

--- a/solution.py
+++ b/solution.py
@@ -361,6 +361,17 @@
         now = cols_ref[kp].reshape(2048, 256)
         block = invert_block(quarters(dot(now, now, TN)))
 
+        @pl.when((t >= 2) & (order(t - 1 + (1 - (t + 11) // 12)) < 8))
+        def _():
+            due = order(t - 1) + 4
+            arrive(first(due))
+            go(second(due))
+
+        @pl.when(t == 2)
+        def _():
+            arrive(first(4))
+            go(second(4))
+
         @pl.when((t >= 3) & (order(t - 2 + 2 * (1 - (t + 10) // 12)) < 8))
         def _():
             due = order(t - 2) + 4
@@ -371,17 +382,6 @@
         def _():
             arrive(second(4))
             go(third(4))
-
-        @pl.when((t >= 2) & (order(t - 1 + (1 - (t + 11) // 12)) < 8))
-        def _():
-            due = order(t - 1) + 4
-            arrive(first(due))
-            go(second(due))
-
-        @pl.when(t == 2)
-        def _():
-            arrive(first(4))
-            go(second(4))
 
         high, low = split(block)
         weights = jnp.concatenate(

time: 181 us -> 181 us (level)
  no operation moved by 1% of the time
where the time goes in v6:
time: 181 us; the launch traced here: 179 us
  Pallas kernels  179 us (99%)
    pallas_call x1, Pallas kernels, local(): pl.pallas_call(kernel, out_shape=shapes, in_specs=[VM, VM, pl.BlockSpec(m...  177 us

profile of v6, /device:TPU:1, one launch (start us, length us, event | category | flops | bytes accessed | tf_op | source)
XLA Modules:
  0.0 179.4 jit_solution(901656358014254957)
XLA Ops:
  0.6 177.1 %shard_map.68 = (f32[128,512]{1,0:T(8,128)}, f32[32,512]{1,0:T(8,128)}) custom-call(bf16[512,512]{1,0:T(8,128)(2,1)} %st_ref.1, f32[1,512]{1,0:T(1,128)} %bitcast.3, bf16[512,2048]{1,0:T(8,128)(2,1)} %w_any.1, f32[1,128]{1,0:T(1,128)} %bitcast.4, s32[128,512]{1,0:T(8,128)} %sketch_ref.1), custom_call_target="tpu_custom_call" | custom-call | tf_op jit(solution)/shard_map/pallas_call | solution.py:450
  177.8 1.7 shard_map.69
